TPU v7x, 32 devices: a whole 2x2x4 slice. The times are simulated.
32 devices in a mesh: parts: 2 (over y), blk: 8 (over z, x), dp: 2 (over core).
Axes of the slice: x: 2, y: 2, z: 4, core: 2. Of those that a mesh axis runs over, the one named last changes fastest.
Arguments:
- activations: bfloat16 [4, 176, 14336], P(('parts', 'dp'), None, 'blk'), parts along dimension 0, may hold values from -6 to 6
- out_grads: bfloat16 [4, 176, 4096], P(('parts', 'dp'), None, 'blk'), parts along dimension 0, may hold values from -6 to 6
- input_basis: bfloat16 [28672, 14336], P('parts', 'blk'), parts along dimension 0, may hold values from -0.046875 to 0.046875
- output_basis: bfloat16 [8192, 4096], P('parts', 'blk'), parts along dimension 0, may hold values from -0.09375 to 0.09375
Outputs:
- correction: float32 [8192, 14336], P(('parts', 'dp'), 'blk'), parts along dimension 0
There are 2 independent parts, one for each index of `parts`. A program takes and returns all parts, laid end to end along the dimension named above; each array names one. Nothing has to cross between parts.
All inputs are finite; a program needn't handle non-finite values.
Results may differ from a plain program's by a relative error of at most 0.0042.
Values may be sent and summed in bfloat16 or wider, within the bound.
No kernel may reach another device: no remote copies, remote signals or barrier semaphores. Data moves between devices by JAX's collectives and lax.ppermute only.
A program may use at most 256 MiB of HBM per device.

v0:
```python
import math

import jax
import jax.numpy as jnp
from jax import lax
from jax.sharding import PartitionSpec as P


def body(activations, out_grads, input_basis, output_basis):
    seq_dev, length, in_local = activations.shape
    out_local = out_grads.shape[2]
    tokens = seq_dev * length
    slab_width = input_basis.shape[1]
    panel_width = output_basis.shape[1]
    flat_inputs = activations.reshape(tokens, in_local)
    flat_grads = out_grads.reshape(tokens, out_local)
    basis_rows = input_basis
    summed_in = jnp.dot(
        lax.all_gather(flat_inputs, "blk", axis=1, tiled=True),
        basis_rows,
        preferred_element_type=jnp.float32,
    )
    basis_rows = output_basis
    summed_out = jnp.dot(
        lax.all_gather(flat_grads, "blk", axis=1, tiled=True),
        basis_rows,
        preferred_element_type=jnp.float32,
    )
    rotated_in = summed_in.astype(jnp.bfloat16).reshape(seq_dev, length, slab_width)
    rotated_out = summed_out.astype(jnp.bfloat16).reshape(seq_dev, length, panel_width)
    factor = 1.0 / math.sqrt(length)
    data_count = lax.axis_size("dp")
    tiles = (
        jnp.einsum(
            "slp,slj->spj",
            lax.all_gather(rotated_out, "blk", axis=2, tiled=True),
            rotated_in,
            preferred_element_type=jnp.float32,
        )
        * factor
    )
    partial_value = jnp.sum(tiles * tiles, axis=0)
    summed = lax.psum_scatter(partial_value, "dp", scatter_dimension=0, tiled=True)
    return summed / (seq_dev * data_count)


def solution(mesh):
    placed = (
        P(("parts", "dp"), None, "blk"),
        P(("parts", "dp"), None, "blk"),
        P("parts", "blk"),
        P("parts", "blk"),
    )
    return jax.shard_map(
        body, mesh=mesh, in_specs=placed, out_specs=P(("parts", "dp"), "blk"), check_vma=False
    )
```

profile of v0, /device:TPU:1, one launch (start us, length us, event | category | flops | bytes accessed | tf_op | source)
XLA Modules:
  0.0 254.6 jit_solution(1416203112301035645)
XLA Ops:
  6.5 0.0 all-gather.7.cloned.1.call-start
  6.5 0.7 all-gather.7.cloned.1.call-update
  7.3 0.0 all-gather.11.cloned.1.call-start
  7.3 0.7 all-gather.11.cloned.1.call-update
  8.0 0.0 all-gather.9.cloned.1.call-start
  8.1 44.4 %all-gather.7.cloned.1.call-done = bf16[1,176,4096]{2,1,0:T(8,128)(2,1)} async-done(((bf16[1,176,512]{2,1,0:T(8,128)(2,1)}), bf16[1,176,4096]{2,1,0:T(8,128)(2,1)}) %all-gather.7.cloned.1.call-update) | async-done | bytes 1441808 | tf_op jit(solution)/shard_map/all_gather | solution.py:25
  52.5 4.2 %fusion.7 = bf16[176,512]{1,0:T(8,128)(2,1)} fusion(bf16[4096,512]{1,0:T(8,128)(2,1)} %param.7, bf16[1,176,4096]{2,1,0:T(8,128)(2,1)} %all-gather.7.cloned.1.call-done), kind=kOutput, calls=%fused_computation.7 | convolution fusion | flops 738287616 | bytes 5816320 | tf_op jit(solution)/shard_map/dot_general | solution.py:24
  56.7 0.0 all-gather.9.cloned.1.call-update
  56.7 0.0 reduce-scatter.2.cloned.1.call-start
  56.7 81.8 %all-gather.11.cloned.1.call-done = bf16[1,176,14336]{2,1,0:T(8,128)(2,1)} async-done(((bf16[1,176,1792]{2,1,0:T(8,128)(2,1)}), bf16[1,176,14336]{2,1,0:T(8,128)(2,1)}) %all-gather.11.cloned.1.call-update) | async-done | bytes 5046288 | tf_op jit(solution)/shard_map/all_gather | solution.py:19
  138.5 20.9 %fusion.2 = bf16[176,1792]{1,0:T(8,128)(2,1)S(1)} fusion(bf16[14336,1792]{1,0:T(8,128)(2,1)} %param.6, bf16[1,176,14336]{2,1,0:T(8,128)(2,1)} %all-gather.11.cloned.1.call-done), kind=kOutput, calls=%fused_computation.4 | convolution fusion | flops 9043234816 | bytes 57057280 | tf_op jit(solution)/shard_map/dot_general | solution.py:18
  159.4 21.7 %all-gather.9.cloned.1.call-done = bf16[176,4096]{1,0:T(8,128)(2,1)} async-done(((bf16[176,512]{1,0:T(8,128)(2,1)}), bf16[176,4096]{1,0:T(8,128)(2,1)}) %all-gather.9.cloned.1.call-update) | async-done | bytes 1441808 | tf_op jit(solution)/shard_map/all_gather | solution.py:36
  181.0 13.4 %multiply_multiply_fusion = f32[4096,1792]{1,0:T(8,128)} fusion(bf16[176,4096]{1,0:T(8,128)(2,1)} %all-gather.9.cloned.1.call-done, bf16[176,1792]{1,0:T(8,128)(2,1)S(1)} %fusion.2), kind=kOutput, calls=%fused_computation | convolution fusion | flops 2598371328 | bytes 31432704 | tf_op jit(solution)/shard_map/slp,slj->spj/dot_general | solution.py:34
  194.4 0.0 reduce-scatter.2.cloned.1.call-update
  194.4 42.1 %reduce-scatter.2.cloned.1.call-done = f32[2048,1792]{1,0:T(8,128)} async-done(((f32[4096,1792]{1,0:T(8,128)}), f32[2048,1792]{1,0:T(8,128)}) %reduce-scatter.2.cloned.1.call-update) | async-done | bytes 14680080 | tf_op jit(solution)/shard_map/reduce_scatter | solution.py:43
  236.5 11.6 %broadcast_multiply_fusion = f32[2048,1792]{1,0:T(8,128)} fusion(f32[2048,1792]{1,0:T(8,128)} %reduce-scatter.2.cloned.1.call-done), kind=kLoop, calls=%fused_computation.1 | loop fusion | flops 3670016 | bytes 29360128 | tf_op jit(solution)/shard_map/div | solution.py:44
Async XLA Ops:
  6.5 45.9 %all-gather.7.cloned.1.call-start = ((), (), s32[]{:S(2)}) async-start(), calls=%async_computation.2 | async-start | bytes 1622016 | tf_op jit(solution)/shard_map/all_gather | solution.py:25
  7.3 131.2 %all-gather.11.cloned.1.call-start = ((), (), s32[]{:S(2)}) async-start(), calls=%async_computation.4 | async-start | bytes 5677056 | tf_op jit(solution)/shard_map/all_gather | solution.py:19
  8.0 173.0 %all-gather.9.cloned.1.call-start = ((), (), s32[]{:S(2)}) async-start(), calls=%async_computation.3 | async-start | bytes 1622016 | tf_op jit(solution)/shard_map/all_gather | solution.py:36
  56.7 179.8 %reduce-scatter.2.cloned.1.call-start = ((), (), s32[]{:S(2)}) async-start(), calls=%async_computation.1 | async-start | bytes 44040192 | tf_op jit(solution)/shard_map/reduce_scatter | solution.py:43
Sparse Core Ops, SparseCore 0:
  9.4 43.0 all-gather.6
  54.7 83.7 all-gather.10
  140.5 40.4 all-gather.8
  194.5 41.9 reduce-scatter.1
where the time goes:
time: 255 us
  waiting for transfers between devices  191 us (75%)
  matrix products  38.5 us (15%)
  between operations  13.1 us (5%)
  other arithmetic  11.6 us (5%)
    all_gather x1, waiting for transfers between devices, body(): lax.all_gather(flat_inputs, 'blk', axis=1, tiled=True)  81.8 us
    all_gather x1, waiting for transfers between devices, body(): lax.all_gather(flat_grads, 'blk', axis=1, tiled=True)  44.4 us
    reduce_scatter x1, waiting for transfers between devices, body(): lax.psum_scatter(partial_value, 'dp', scatter_dimension=0, tiled=True)  42.1 us
    all_gather x1, waiting for transfers between devices, body(): lax.all_gather(rotated_out, 'blk', axis=2, tiled=True)  21.7 us
    dot_general x1, matrix products, body(): jnp.dot(lax.all_gather(flat_inputs, 'blk', axis=1, tiled=True), basis_row...  20.9 us
    dot_general x1, matrix products, body(): jnp.einsum('slp,slj->spj', lax.all_gather(rotated_out, 'blk', axis=2, til...  13.4 us
    div x1, other arithmetic, body(): return summed / (seq_dev * data_count)  11.6 us
  transfers between devices with their start and end apart: 4, of which 4 were waited for; matrix products, arithmetic and copies ran while one was open for 10% of the time, Pallas kernels for 0%

commit v1 on v0

v1 whole, which is shorter than its diff:
```python
import math

import jax
import jax.numpy as jnp
from jax import lax
from jax.experimental import pallas as pl
from jax.experimental.pallas import tpu as pltpu
from jax.sharding import PartitionSpec as P

SWAP = ((0, 1), (1, 0))
SLAB = 448


def chunk_at(n, q):
    q = lax.rem(q + 2 * n, n)
    return jnp.where(q < n // 2, 2 * q, 2 * n - 1 - 2 * q)


def place_of(n, me):
    return jnp.where(lax.rem(me, 2) == 0, me // 2, n - 1 - me // 2)


def rotate(pieces, distances, offsets, basis, running, last):
    count = len(pieces)
    tokens = pieces[0].shape[0]
    columns = basis.shape[1]
    n = lax.axis_size("blk")
    chunk_rows = basis.shape[0] // n
    slabs = []
    row = 0
    for k in range(count):
        width = pieces[k].shape[1]
        size = SLAB if width % SLAB == 0 else width
        for begin in range(0, width, size):
            slabs.append((k, begin, size, row))
            row += size
    total = row
    has_running = running is not None
    steps = len(slabs)

    def kernel(*refs):
        xs, basis_ref, refs = refs[:count], refs[count], refs[count + 1 :]
        if has_running:
            run_ref, refs = refs[0], refs[1:]
        out_ref, refs = refs[0], refs[1:]
        held, refs = refs[:count], refs[count:]
        slab, acc, sems = refs
        place = place_of(n, lax.axis_index("blk"))
        brought = [pltpu.make_async_copy(xs[k], held[k], sems.at[steps + k]) for k in range(count)]
        copies = []
        for i, (k, begin, size, row) in enumerate(slabs):
            if begin == 0:
                brought[k].start()
            start = pl.multiple_of(chunk_at(n, place + distances[k]) * chunk_rows + offsets[k] + begin, 64)
            copy = pltpu.make_async_copy(basis_ref.at[pl.ds(start, size), :], slab.at[row : row + size, :], sems.at[i])
            copy.start()
            copies.append(copy)
        if has_running:
            run_copy = pltpu.make_async_copy(run_ref, acc, sems.at[steps + count])
            run_copy.start()
        for i, (k, begin, size, row) in enumerate(slabs):
            if begin == 0:
                brought[k].wait()
            copies[i].wait()
            value = jnp.dot(held[k][:, begin : begin + size], slab[row : row + size, :], preferred_element_type=jnp.float32)
            if i == 0 and has_running:
                run_copy.wait()
            if i > 0 or has_running:
                value = acc[...] + value
            if i < steps - 1:
                acc[...] = value
            else:
                out_ref[...] = value.astype(out_ref.dtype)

    whole = pl.BlockSpec(memory_space=pltpu.VMEM)
    anywhere = pl.BlockSpec(memory_space=pl.ANY)
    planned = 2 * total * (columns + tokens) + 8 * tokens * columns
    return pl.pallas_call(
        kernel,
        out_shape=jax.ShapeDtypeStruct((tokens, columns), jnp.bfloat16 if last else jnp.float32),
        in_specs=[anywhere] * (count + 1 + has_running),
        out_specs=whole,
        scratch_shapes=[pltpu.VMEM(p.shape, p.dtype) for p in pieces]
        + [
            pltpu.VMEM((total, columns), basis.dtype),
            pltpu.VMEM((tokens, columns), jnp.float32),
            pltpu.SemaphoreType.DMA((steps + count + 1,)),
        ],
        compiler_params=pltpu.CompilerParams(vmem_limit_bytes=planned + 8 * 1024 * 1024),
        cost_estimate=pl.CostEstimate(
            flops=2 * tokens * total * columns, bytes_accessed=2 * total * columns + 8 * tokens * columns, transcendentals=0
        ),
    )(*pieces, basis, *([running] if has_running else []))


def square_tiles(pieces, distances, offsets, in_mine, in_other, shape, scale, before):
    count = len(pieces)
    tokens, columns = in_mine.shape
    widths = [p[0].shape[1] for p in pieces]
    total = sum(widths)
    has_before = before is not None
    n = lax.axis_size("blk")
    rows_local = shape[0]
    chunk_rows = 2 * rows_local // n
    size = 128

    def kernel(*refs):
        outs, refs = refs[: 2 * count], refs[2 * count :]
        mine_ref, other_ref, refs = refs[0], refs[1], refs[2:]
        if has_before:
            refs = refs[1:]
        out_ref, held, sems = refs
        place = place_of(n, lax.axis_index("blk"))
        starts = [chunk_at(n, place + distances[k]) * chunk_rows + offsets[k] - lax.axis_index("dp") * rows_local for k in range(count)]
        valid = [(start >= 0) & (start < rows_local) for start in starts]

        def copies(k, row):
            start = pl.multiple_of(jnp.where(valid[k], starts[k], 0), size)
            return [
                pltpu.make_async_copy(
                    held.at[pl.ds(row + i * size, size), :], out_ref.at[pl.ds(start + i * size, size), :], sems.at[row // size + i]
                )
                for i in range(widths[k] // size)
            ]

        row = 0
        for k in range(count):

            @pl.when(valid[k])
            def _(k=k, row=row):
                for i, copy in enumerate(copies(k, row)):
                    cols = slice(i * size, (i + 1) * size)
                    first, second = [
                        lax.dot_general(x[:, cols], y[...], (((0,), (0,)), ((), ())), preferred_element_type=jnp.float32)
                        for x, y in ((outs[2 * k], mine_ref), (outs[2 * k + 1], other_ref))
                    ]
                    held[row + i * size : row + (i + 1) * size, :] = (first * first + second * second) * scale
                    copy.start()

            row += widths[k]
        row = 0
        for k in range(count):

            @pl.when(valid[k])
            def _(k=k, row=row):
                for copy in copies(k, row):
                    copy.wait()

            row += widths[k]

    whole = pl.BlockSpec(memory_space=pltpu.VMEM)
    anywhere = pl.BlockSpec(memory_space=pl.ANY)
    return pl.pallas_call(
        kernel,
        out_shape=jax.ShapeDtypeStruct(shape, jnp.float32),
        in_specs=[whole] * (2 * count + 2) + [anywhere] * has_before,
        out_specs=anywhere,
        scratch_shapes=[
            pltpu.VMEM((total, columns), jnp.float32),
            pltpu.SemaphoreType.DMA((total // size,)),
        ],
        input_output_aliases={2 * count + 2: 0} if has_before else {},
        compiler_params=pltpu.CompilerParams(vmem_limit_bytes=4 * total * columns + 16 * 1024 * 1024),
        cost_estimate=pl.CostEstimate(
            flops=2 * tokens * total * columns, bytes_accessed=2 * total * columns, transcendentals=0
        ),
    )(*[x for p in pieces for x in p], in_mine, in_other, *([before] if has_before else []))


def ring_body(activations, out_grads, input_basis, output_basis):
    _, length, in_width = activations.shape
    out_width = out_grads.shape[2]
    acts = activations[0]
    grads = out_grads[0]
    n = lax.axis_size("blk")
    rows_local = n * out_width // 2
    half_in, half_out = in_width // 2, out_width // 2

    path = [2 * q if q < n // 2 else 2 * n - 1 - 2 * q for q in range(n)]
    ahead = [(path[i], path[(i + 1) % n]) for i in range(n)]
    back = [(path[i], path[(i - 1) % n]) for i in range(n)]

    def hop(forward, backward, *after):
        if after:
            forward, backward, _ = lax.optimization_barrier((forward, backward, after))
        return lax.ppermute(forward, "blk", ahead), lax.ppermute(backward, "blk", back)

    def add(total, got, distance):
        return rotate(list(got), (-distance, distance), (0, 0), input_basis, total, False)

    def swap(x):
        return lax.ppermute(x, "dp", SWAP)

    g1 = hop(grads, grads)
    a1 = hop(acts, acts)
    total = rotate([acts], (0,), (0,), input_basis, None, False)
    g2 = hop(*g1, total)
    g3 = hop(*g2)
    a2 = hop(*a1, g2)
    total = add(total, a1, 1)
    g4 = hop(g3[0][:, :half_out], g3[1][:, half_out:], total)
    rotated_out = rotate(
        [grads, *g1, *g2, *g3, *g4], (0, -1, 1, -2, 2, -3, 3, -4, 4), (0,) * 8 + (half_out,), output_basis, None, True
    )
    r1 = hop(rotated_out, rotated_out)
    a3 = hop(*a2, g4)
    total = add(total, a2, 2)
    r2 = hop(*r1, total)
    a4 = hop(a3[0][:, :half_in], a3[1][:, half_in:], r1)
    total = add(total, a3, 3)
    r3 = hop(*r2, total)
    rotated_in = rotate(list(a4), (-4, 4), (0, half_in), input_basis, total, True)
    r4 = hop(r3[0][:, :half_out], r3[1][:, half_out:], rotated_in)
    other_in = swap(rotated_in)
    scale = 1.0 / (length * 2)

    def tiles(pieces, distances, offsets, before):
        pairs = [(p, swap(p)) for p in pieces]
        return square_tiles(pairs, distances, offsets, rotated_in, other_in, (rows_local, in_width), scale, before)

    out = tiles([rotated_out, *r1, *r2], (0, -1, 1, -2, 2), (0,) * 5, None)
    return tiles([*r3, *r4], (-3, 3, -4, 4), (0, 0, 0, half_out), out)


def gather_body(activations, out_grads, input_basis, output_basis):
    seqs, length, _ = activations.shape

    def rotated(x, basis):
        whole = lax.all_gather(x, "blk", axis=2, tiled=True)
        return jnp.einsum("slk,kj->slj", whole, basis, preferred_element_type=jnp.float32).astype(jnp.bfloat16)

    rotated_in = rotated(activations, input_basis)
    rotated_out = lax.all_gather(rotated(out_grads, output_basis), "blk", axis=2, tiled=True)
    tile = jnp.einsum("slp,slj->spj", rotated_out, rotated_in, preferred_element_type=jnp.float32)
    squares = jnp.sum(tile * tile, axis=0)
    summed = lax.psum_scatter(squares, "dp", scatter_dimension=0, tiled=True)
    return summed * (1.0 / (length * seqs * lax.axis_size("dp")))


def solution(mesh):
    placed = (
        P(("parts", "dp"), None, "blk"),
        P(("parts", "dp"), None, "blk"),
        P("parts", "blk"),
        P("parts", "blk"),
    )
    ring = mesh.shape["blk"] == 8 and mesh.shape["dp"] == 2
    body = ring_body if ring else gather_body
    return jax.shard_map(
        body, mesh=mesh, in_specs=placed, out_specs=P(("parts", "dp"), "blk"), check_vma=False
    )
```

time: 255 us -> 125 us (0.49)
  waiting for transfers between devices: 191 us -> 52.1 us
  matrix products: 38.5 us -> 0 us
  Pallas kernels: 0 us -> 36.4 us
  starting transfers between devices: 0.12 us -> 35.2 us
  between operations: 13.1 us -> 0.35 us
  other arithmetic: 11.6 us -> 0 us
    all_gather x3 -> x0, waiting for transfers between devices: 148 us -> none  [the longest x1 81.8 us: body(): lax.all_gather(flat_inputs, 'blk', axis=1, tiled=True)]
    ppermute x0 -> x34, waiting for transfers between devices: none -> 52.1 us  [the longest x12 31.1 us: hop(): lax.ppermute(forward, 'blk', ahead)]
    reduce_scatter x1 -> x0, waiting for transfers between devices: 42.1 us -> none  [body(): lax.psum_scatter(partial_value, 'dp', scatter_dimension=0, tiled=True)]
    dot_general x3 -> x0, matrix products: 38.5 us -> none  [the longest x1 20.9 us: body(): jnp.dot(lax.all_gather(flat_inputs, 'blk', axis=1, tiled=True), basis_row...]
    pallas_call x0 -> x8, Pallas kernels: none -> 36.4 us  [the longest x6 29.2 us: rotate(): pl.pallas_call(kernel, out_shape=jax.ShapeDtypeStruct((tokens, columns),...]
    ppermute x0 -> x34, starting transfers between devices: none -> 35.2 us  [the longest x10 16.7 us: swap(): return lax.ppermute(x, 'dp', SWAP)]
    div x1 -> x0, other arithmetic: 11.6 us -> none  [body(): return summed / (seq_dev * data_count)]
  transfers between devices with their start and end apart: 4 -> 34, of which waited for: 4 -> 15; matrix products, arithmetic and copies ran while one was open for 10% -> 0% of each run, Pallas kernels for 0% -> 22%
where the time goes in v1:
time: 125 us
  waiting for transfers between devices  52.1 us (42%)
  Pallas kernels  36.4 us (29%)
  starting transfers between devices  35.2 us (28%)
    ppermute x12, waiting for transfers between devices, hop(): lax.ppermute(forward, 'blk', ahead)  31.1 us
    pallas_call x6, Pallas kernels, rotate(): pl.pallas_call(kernel, out_shape=jax.ShapeDtypeStruct((tokens, columns),...  29.2 us
    ppermute x12, waiting for transfers between devices, hop(): lax.ppermute(backward, 'blk', back)  20.9 us
    ppermute x10, starting transfers between devices, swap(): return lax.ppermute(x, 'dp', SWAP)  16.7 us
    ppermute x12, starting transfers between devices, hop(): lax.ppermute(forward, 'blk', ahead)  10.2 us
    ppermute x12, starting transfers between devices, hop(): lax.ppermute(backward, 'blk', back)  8.38 us
    pallas_call x2, Pallas kernels, square_tiles(): pl.pallas_call(kernel, out_shape=jax.ShapeDtypeStruct(shape, jnp.float32)...  7.25 us
  transfers between devices with their start and end apart: 34, of which 15 were waited for; matrix products, arithmetic and copies ran while one was open for 0% of the time, Pallas kernels for 22%

profile of v1, /device:TPU:1, one launch (start us, length us, event | category | flops | bytes accessed | tf_op | source)
XLA Modules:
  0.0 125.2 jit_solution(11487155692468308072)
XLA Ops:
  0.0 2.0 %collective-permute-start.7 = (bf16[176,1792]{1,0:T(8,128)(2,1)}, bf16[176,1792]{1,0:T(8,128)(2,1)S(1)}, u32[]{:S(2)}, u32[]{:S(2)}) collective-permute-start(bf16[176,1792]{1,0:T(8,128)(2,1)} %bitcast.2), channel_id=1, source_target_pairs={{0,2},{4,0},{8,4},{12,8},{14,12},{10,14},{6,10},{2,6},{1,3},{5,1},... | collective-permute-start | bytes 1892360 | tf_op jit(solution)/shard_map/ppermute | solution.py:186
  2.1 1.4 %collective-permute-start.1 = (bf16[176,512]{1,0:T(8,128)(2,1)}, bf16[176,512]{1,0:T(8,128)(2,1)S(1)}, u32[]{:S(2)}, u32[]{:S(2)}) collective-permute-start(bf16[176,512]{1,0:T(8,128)(2,1)} %bitcast.5), channel_id=1, source_target_pairs={{0,2},{4,0},{8,4},{12,8},{14,12},{10,14},{6,10},{2,6},{1,3},{5,1},... | collective-permute-start | bytes 540680 | tf_op jit(solution)/shard_map/ppermute | solution.py:186
  4.7 3.6 %shard_map.46.refs_3_ = f32[176,1792]{1,0:T(8,128)S(1)} custom-call(bf16[176,1792]{1,0:T(8,128)(2,1)S(1)} %bitcast.4, bf16[14336,1792]{1,0:T(8,128)(2,1)} %refs_2_.7), custom_call_target="tpu_custom_call" | custom-call | flops 1130364928 | bytes 8945664 | tf_op jit(solution)/shard_map/pallas_call | solution.py:78
  8.3 11.8 %collective-permute-done.1.refs_2_ = bf16[176,512]{1,0:T(8,128)(2,1)S(1)} collective-permute-done((bf16[176,512]{1,0:T(8,128)(2,1)}, bf16[176,512]{1,0:T(8,128)(2,1)S(1)}, u32[]{:S(2)}, u32[]{:S(2)}) %collective-permute-start.1) | collective-permute-done | bytes 180256 | tf_op jit(solution)/shard_map/ppermute | solution.py:186
  22.3 2.9 %collective-permute-done.2.refs_3_ = bf16[176,512]{1,0:T(8,128)(2,1)S(1)} collective-permute-done((bf16[176,512]{1,0:T(8,128)(2,1)S(1)}, bf16[176,512]{1,0:T(8,128)(2,1)S(1)}, u32[]{:S(2)}, u32[]{:S(2)}) %collective-permute-start.2) | collective-permute-done | bytes 180256 | tf_op jit(solution)/shard_map/ppermute | solution.py:186
  28.9 13.9 %collective-permute-done.4.refs_5_ = bf16[176,512]{1,0:T(8,128)(2,1)S(1)} collective-permute-done((bf16[176,512]{1,0:T(8,128)(2,1)S(1)}, bf16[176,512]{1,0:T(8,128)(2,1)S(1)}, u32[]{:S(2)}, u32[]{:S(2)}) %collective-permute-start.4) | collective-permute-done | bytes 180256 | tf_op jit(solution)/shard_map/ppermute | solution.py:186
  43.7 6.1 %shard_map.47.refs_3_ = f32[176,1792]{1,0:T(8,128)S(1)} custom-call(bf16[176,1792]{1,0:T(8,128)(2,1)S(1)} %collective-permute-done.6.refs_0_, bf16[176,1792]{1,0:T(8,128)(2,1)S(1)} %collective-permute-done.7.refs_1_, bf16[14336,1792]{1,0:T(8,128)(2,1)} %refs_2_.7, f32[176,1792]{1,0:T(8,128)S(1)} %shard_map.46.refs_3_), custom_call_target="tpu_custom_call" | custom-call | flops 2260729856 | bytes 15368192 | tf_op jit(solution)/shard_map/pallas_call | solution.py:78
  49.8 1.3 %collective-permute-start.8 = (bf16[176,256]{1,0:T(8,128)(2,1)S(1)}, bf16[176,256]{1,0:T(8,128)(2,1)S(1)}, u32[]{:S(2)}, u32[]{:S(2)}) collective-permute-start(bf16[176,256]{1,0:T(8,128)(2,1)S(1)} %slice.24), channel_id=1, source_target_pairs={{0,4},{4,8},{8,12},{12,14},{14,10},{10,6},{6,2},{2,0},{1,5},{5,9},... | collective-permute-start | bytes 270344 | tf_op jit(solution)/shard_map/ppermute | solution.py:186
  51.3 1.9 %collective-permute-done.8.refs_7_ = bf16[176,256]{1,0:T(8,128)(2,1)S(1)} collective-permute-done((bf16[176,256]{1,0:T(8,128)(2,1)S(1)}, bf16[176,256]{1,0:T(8,128)(2,1)S(1)}, u32[]{:S(2)}, u32[]{:S(2)}) %collective-permute-start.8) | collective-permute-done | bytes 90144 | tf_op jit(solution)/shard_map/ppermute | solution.py:186
  56.0 3.7 %shard_map.48.refs_0_ = bf16[176,512]{1,0:T(8,128)(2,1)S(1)} custom-call(bf16[176,512]{1,0:T(8,128)(2,1)S(1)} %bitcast.7, bf16[176,512]{1,0:T(8,128)(2,1)S(1)} %collective-permute-done.refs_1_, bf16[176,512]{1,0:T(8,128)(2,1)S(1)} %collective-permute-done.1.refs_2_, bf16[176,512]{1,0:T(8,128)(2,1)S(1)} %collective-permute-done.2.refs_3_, ...), custom_call_target="tpu_custom_call" | custom-call | flops 738197504 | bytes 4915200 | tf_op jit(solution)/shard_map/pallas_call | solution.py:78
  61.2 4.2 %collective-permute-done.16.refs_0_ = bf16[176,1792]{1,0:T(8,128)(2,1)S(1)} collective-permute-done((bf16[176,1792]{1,0:T(8,128)(2,1)S(1)}, bf16[176,1792]{1,0:T(8,128)(2,1)S(1)}, u32[]{:S(2)}, u32[]{:S(2)}) %collective-permute-start.16) | collective-permute-done | bytes 630816 | tf_op jit(solution)/shard_map/ppermute | solution.py:186
  66.6 3.8 %collective-permute-done.11.refs_4_ = bf16[176,512]{1,0:T(8,128)(2,1)S(1)} collective-permute-done((bf16[176,512]{1,0:T(8,128)(2,1)S(1)}, bf16[176,512]{1,0:T(8,128)(2,1)S(1)}, u32[]{:S(2)}, u32[]{:S(2)}) %collective-permute-start.11) | collective-permute-done | bytes 180256 | tf_op jit(solution)/shard_map/ppermute | solution.py:186
  71.9 6.0 %shard_map.49.refs_3_ = f32[176,1792]{1,0:T(8,128)S(1)} custom-call(bf16[176,1792]{1,0:T(8,128)(2,1)S(1)} %collective-permute-done.12.refs_0_, bf16[176,1792]{1,0:T(8,128)(2,1)S(1)} %collective-permute-done.13.refs_1_, bf16[14336,1792]{1,0:T(8,128)(2,1)} %refs_2_.7, f32[176,1792]{1,0:T(8,128)S(1)} %shard_map.47.refs_3_), custom_call_target="tpu_custom_call" | custom-call | flops 2260729856 | bytes 15368192 | tf_op jit(solution)/shard_map/pallas_call | solution.py:78
  77.9 6.0 %shard_map.50.refs_3_ = f32[176,1792]{1,0:T(8,128)S(1)} custom-call(bf16[176,1792]{1,0:T(8,128)(2,1)S(1)} %collective-permute-done.16.refs_0_, bf16[176,1792]{1,0:T(8,128)(2,1)S(1)} %collective-permute-done.17.refs_1_, bf16[14336,1792]{1,0:T(8,128)(2,1)} %refs_2_.7, f32[176,1792]{1,0:T(8,128)S(1)} %shard_map.49.refs_3_), custom_call_target="tpu_custom_call" | custom-call | flops 2260729856 | bytes 15368192 | tf_op jit(solution)/shard_map/pallas_call | solution.py:78
  83.9 3.8 %shard_map.51.refs_10_.refs_8_ = bf16[176,1792]{1,0:T(8,128)(2,1)S(1)} custom-call(bf16[176,896]{1,0:T(8,128)(2,1)S(1)} %collective-permute-done.22.refs_0_, bf16[176,896]{1,0:T(8,128)(2,1)S(1)} %collective-permute-done.23.refs_1_, bf16[14336,1792]{1,0:T(8,128)(2,1)} %refs_2_.7, f32[176,1792]{1,0:T(8,128)S(1)} %shard_map.50.refs_3_), custom_call_target="tpu_custom_call" | custom-call | flops 1130364928 | bytes 8945664 | tf_op jit(solution)/shard_map/pallas_call | solution.py:78
  87.7 9.9 %collective-permute-start.28 = (bf16[176,1792]{1,0:T(8,128)(2,1)S(1)}, bf16[176,1792]{1,0:T(8,128)(2,1)S(1)}, u32[]{:S(2)}, u32[]{:S(2)}) collective-permute-start(bf16[176,1792]{1,0:T(8,128)(2,1)S(1)} %shard_map.51.refs_10_.refs_8_), channel_id=1, source_target_pairs={{0,1},{1,0},{2,3},{3,2},{4,5},{5,4},{6,7},{7,6},{8,9},{9,8},{10,11... | collective-permute-start | bytes 1892360 | tf_op jit(solution)/shard_map/ppermute | solution.py:192
  97.6 1.6 %collective-permute-start.14 = (bf16[176,512]{1,0:T(8,128)(2,1)S(1)}, bf16[176,512]{1,0:T(8,128)(2,1)S(1)}, u32[]{:S(2)}, u32[]{:S(2)}) collective-permute-start(bf16[176,512]{1,0:T(8,128)(2,1)S(1)} %collective-permute-done.10.refs_2_), channel_id=1, source_target_pairs={{0,4},{4,8},{8,12},{12,14},{14,10},{10,6},{6,2},{2,0},{1,5},{5,9},... | collective-permute-start | bytes 540680 | tf_op jit(solution)/shard_map/ppermute | solution.py:186
  99.7 4.0 %collective-permute-done.14.refs_6_ = bf16[176,512]{1,0:T(8,128)(2,1)S(1)} collective-permute-done((bf16[176,512]{1,0:T(8,128)(2,1)S(1)}, bf16[176,512]{1,0:T(8,128)(2,1)S(1)}, u32[]{:S(2)}, u32[]{:S(2)}) %collective-permute-start.14) | collective-permute-done | bytes 180256 | tf_op jit(solution)/shard_map/ppermute | solution.py:186
  106.5 1.7 %collective-permute-start.31 = (bf16[176,512]{1,0:T(8,128)(2,1)S(1)}, bf16[176,512]{1,0:T(8,128)(2,1)S(1)}, u32[]{:S(2)}, u32[]{:S(2)}) collective-permute-start(bf16[176,512]{1,0:T(8,128)(2,1)S(1)} %collective-permute-done.11.refs_4_), channel_id=1, source_target_pairs={{0,1},{1,0},{2,3},{3,2},{4,5},{5,4},{6,7},{7,6},{8,9},{9,8},{10,11... | collective-permute-start | bytes 540680 | tf_op jit(solution)/shard_map/ppermute | solution.py:192
  108.2 1.7 %collective-permute-done.18.refs_0_ = bf16[176,512]{1,0:T(8,128)(2,1)S(1)} collective-permute-done((bf16[176,512]{1,0:T(8,128)(2,1)S(1)}, bf16[176,512]{1,0:T(8,128)(2,1)S(1)}, u32[]{:S(2)}, u32[]{:S(2)}) %collective-permute-start.18) | collective-permute-done | bytes 180256 | tf_op jit(solution)/shard_map/ppermute | solution.py:186
  109.9 2.1 %collective-permute-start.32 = (bf16[176,512]{1,0:T(8,128)(2,1)S(1)}, bf16[176,512]{1,0:T(8,128)(2,1)S(1)}, u32[]{:S(2)}, u32[]{:S(2)}) collective-permute-start(bf16[176,512]{1,0:T(8,128)(2,1)S(1)} %collective-permute-done.14.refs_6_), channel_id=1, source_target_pairs={{0,1},{1,0},{2,3},{3,2},{4,5},{5,4},{6,7},{7,6},{8,9},{9,8},{10,11... | collective-permute-start | bytes 540680 | tf_op jit(solution)/shard_map/ppermute | solution.py:192
  114.7 1.8 %collective-permute-done.24.refs_4_ = bf16[176,256]{1,0:T(8,128)(2,1)S(1)} collective-permute-done((bf16[176,256]{1,0:T(8,128)(2,1)S(1)}, bf16[176,256]{1,0:T(8,128)(2,1)S(1)}, u32[]{:S(2)}, u32[]{:S(2)}) %collective-permute-start.24) | collective-permute-done | bytes 90144 | tf_op jit(solution)/shard_map/ppermute | solution.py:186
  117.8 2.4 %shard_map.52.refs_10_ = f32[2048,1792]{1,0:T(8,128)} custom-call(bf16[176,512]{1,0:T(8,128)(2,1)S(1)} %shard_map.48.refs_0_, bf16[176,512]{1,0:T(8,128)(2,1)S(1)} %collective-permute-done.29.refs_1_, bf16[176,512]{1,0:T(8,128)(2,1)S(1)} %collective-permute-done.10.refs_2_, bf16[176,512]{1,0:T(8,128)(2,1)S(1)} %collective-permute-done.30.refs_3_, ...), custom_call_target="tpu_custom_call" | custom-call | flops 1614807040 | bytes 9175040 | tf_op jit(solution)/shard_map/pallas_call | solution.py:153
  120.3 4.8 %shard_map.53 = f32[2048,1792]{1,0:T(8,128)} custom-call(bf16[176,512]{1,0:T(8,128)(2,1)S(1)} %collective-permute-done.18.refs_0_, bf16[176,512]{1,0:T(8,128)(2,1)S(1)} %collective-permute-done.19.refs_1_, bf16[176,512]{1,0:T(8,128)(2,1)S(1)} %collective-permute-done.20.refs_2_, ...), custom_call_target="tpu_custom_call", output_to_operand_aliasing={{}: (10, {})} | custom-call | flops 968884224 | bytes 5505024 | tf_op jit(solution)/shard_map/pallas_call | solution.py:153
  (64 shorter events, 22.4 us)
Async XLA Ops:
  0.0 25.9 %collective-permute-start.7 = (bf16[176,1792]{1,0:T(8,128)(2,1)}, bf16[176,1792]{1,0:T(8,128)(2,1)S(1)}, u32[]{:S(2)}, u32[]{:S(2)}) collective-permute-start(bf16[176,1792]{1,0:T(8,128)(2,1)} %bitcast.2), channel_id=1, source_target_pairs={{0,2},{4,0},{8,4},{12,8},{14,12},{10,14},{6,10},{2,6},{1,3},{5,1},... | collective-permute-start | bytes 1892360 | tf_op jit(solution)/shard_map/ppermute | solution.py:186
  2.0 23.9 %collective-permute-start.6 = (bf16[176,1792]{1,0:T(8,128)(2,1)}, bf16[176,1792]{1,0:T(8,128)(2,1)S(1)}, u32[]{:S(2)}, u32[]{:S(2)}) collective-permute-start(bf16[176,1792]{1,0:T(8,128)(2,1)} %bitcast.3), channel_id=1, source_target_pairs={{0,4},{4,8},{8,12},{12,14},{14,10},{10,6},{6,2},{2,0},{1,5},{5,9},... | collective-permute-start | bytes 1892360 | tf_op jit(solution)/shard_map/ppermute | solution.py:186
  2.1 18.0 %collective-permute-start.1 = (bf16[176,512]{1,0:T(8,128)(2,1)}, bf16[176,512]{1,0:T(8,128)(2,1)S(1)}, u32[]{:S(2)}, u32[]{:S(2)}) collective-permute-start(bf16[176,512]{1,0:T(8,128)(2,1)} %bitcast.5), channel_id=1, source_target_pairs={{0,2},{4,0},{8,4},{12,8},{14,12},{10,14},{6,10},{2,6},{1,3},{5,1},... | collective-permute-start | bytes 540680 | tf_op jit(solution)/shard_map/ppermute | solution.py:186
  3.5 17.4 %collective-permute-start = (bf16[176,512]{1,0:T(8,128)(2,1)}, bf16[176,512]{1,0:T(8,128)(2,1)S(1)}, u32[]{:S(2)}, u32[]{:S(2)}) collective-permute-start(bf16[176,512]{1,0:T(8,128)(2,1)} %bitcast.6), channel_id=1, source_target_pairs={{0,4},{4,8},{8,12},{12,14},{14,10},{10,6},{6,2},{2,0},{1,5},{5,9},... | collective-permute-start | bytes 540680 | tf_op jit(solution)/shard_map/ppermute | solution.py:186
  25.9 28.6 %collective-permute-start.12 = (bf16[176,1792]{1,0:T(8,128)(2,1)S(1)}, bf16[176,1792]{1,0:T(8,128)(2,1)S(1)}, u32[]{:S(2)}, u32[]{:S(2)}) collective-permute-start(bf16[176,1792]{1,0:T(8,128)(2,1)S(1)} %collective-permute-done.6.refs_0_), channel_id=1, source_target_pairs={{0,4},{4,8},{8,12},{12,14},{14,10},{10,6},{6,2},{2,0},{1,5},{5,9},... | collective-permute-start | bytes 1892360 | tf_op jit(solution)/shard_map/ppermute | solution.py:186
  27.2 27.3 %collective-permute-start.13 = (bf16[176,1792]{1,0:T(8,128)(2,1)S(1)}, bf16[176,1792]{1,0:T(8,128)(2,1)S(1)}, u32[]{:S(2)}, u32[]{:S(2)}) collective-permute-start(bf16[176,1792]{1,0:T(8,128)(2,1)S(1)} %collective-permute-done.7.refs_1_), channel_id=1, source_target_pairs={{0,2},{4,0},{8,4},{12,8},{14,12},{10,14},{6,10},{2,6},{1,3},{5,1},... | collective-permute-start | bytes 1892360 | tf_op jit(solution)/shard_map/ppermute | solution.py:186
  27.4 15.4 %collective-permute-start.4 = (bf16[176,512]{1,0:T(8,128)(2,1)S(1)}, bf16[176,512]{1,0:T(8,128)(2,1)S(1)}, u32[]{:S(2)}, u32[]{:S(2)}) collective-permute-start(bf16[176,512]{1,0:T(8,128)(2,1)S(1)} %collective-permute-done.2.refs_3_), channel_id=1, source_target_pairs={{0,4},{4,8},{8,12},{12,14},{14,10},{10,6},{6,2},{2,0},{1,5},{5,9},... | collective-permute-start | bytes 540680 | tf_op jit(solution)/shard_map/ppermute | solution.py:186
  28.7 15.0 %collective-permute-start.5 = (bf16[176,512]{1,0:T(8,128)(2,1)S(1)}, bf16[176,512]{1,0:T(8,128)(2,1)S(1)}, u32[]{:S(2)}, u32[]{:S(2)}) collective-permute-start(bf16[176,512]{1,0:T(8,128)(2,1)S(1)} %collective-permute-done.3.refs_4_), channel_id=1, source_target_pairs={{0,2},{4,0},{8,4},{12,8},{14,12},{10,14},{6,10},{2,6},{1,3},{5,1},... | collective-permute-start | bytes 540680 | tf_op jit(solution)/shard_map/ppermute | solution.py:186
  54.5 10.8 %collective-permute-start.16 = (bf16[176,1792]{1,0:T(8,128)(2,1)S(1)}, bf16[176,1792]{1,0:T(8,128)(2,1)S(1)}, u32[]{:S(2)}, u32[]{:S(2)}) collective-permute-start(bf16[176,1792]{1,0:T(8,128)(2,1)S(1)} %collective-permute-done.12.refs_0_), channel_id=1, source_target_pairs={{0,4},{4,8},{8,12},{12,14},{14,10},{10,6},{6,2},{2,0},{1,5},{5,9},... | collective-permute-start | bytes 1892360 | tf_op jit(solution)/shard_map/ppermute | solution.py:186
  55.7 10.9 %collective-permute-start.17 = (bf16[176,1792]{1,0:T(8,128)(2,1)S(1)}, bf16[176,1792]{1,0:T(8,128)(2,1)S(1)}, u32[]{:S(2)}, u32[]{:S(2)}) collective-permute-start(bf16[176,1792]{1,0:T(8,128)(2,1)S(1)} %collective-permute-done.13.refs_1_), channel_id=1, source_target_pairs={{0,2},{4,0},{8,4},{12,8},{14,12},{10,14},{6,10},{2,6},{1,3},{5,1},... | collective-permute-start | bytes 1892360 | tf_op jit(solution)/shard_map/ppermute | solution.py:186
  59.7 10.7 %collective-permute-start.11 = (bf16[176,512]{1,0:T(8,128)(2,1)S(1)}, bf16[176,512]{1,0:T(8,128)(2,1)S(1)}, u32[]{:S(2)}, u32[]{:S(2)}) collective-permute-start(bf16[176,512]{1,0:T(8,128)(2,1)S(1)} %shard_map.48.refs_0_), channel_id=1, source_target_pairs={{0,2},{4,0},{8,4},{12,8},{14,12},{10,14},{6,10},{2,6},{1,3},{5,1},... | collective-permute-start | bytes 540680 | tf_op jit(solution)/shard_map/ppermute | solution.py:186
  59.9 10.5 %collective-permute-start.10 = (bf16[176,512]{1,0:T(8,128)(2,1)S(1)}, bf16[176,512]{1,0:T(8,128)(2,1)S(1)}, u32[]{:S(2)}, u32[]{:S(2)}) collective-permute-start(bf16[176,512]{1,0:T(8,128)(2,1)S(1)} %shard_map.48.refs_0_), channel_id=1, source_target_pairs={{0,4},{4,8},{8,12},{12,14},{14,10},{10,6},{6,2},{2,0},{1,5},{5,9},... | collective-permute-start | bytes 540680 | tf_op jit(solution)/shard_map/ppermute | solution.py:186
  70.4 13.4 %collective-permute-start.22 = (bf16[176,896]{1,0:T(8,128)(2,1)S(1)}, bf16[176,896]{1,0:T(8,128)(2,1)S(1)}, u32[]{:S(2)}, u32[]{:S(2)}) collective-permute-start(bf16[176,896]{1,0:T(8,128)(2,1)S(1)} %slice.28), channel_id=1, source_target_pairs={{0,4},{4,8},{8,12},{12,14},{14,10},{10,6},{6,2},{2,0},{1,5},{5,9},... | collective-permute-start | bytes 946184 | tf_op jit(solution)/shard_map/ppermute | solution.py:186
  71.3 12.5 %collective-permute-start.23 = (bf16[176,896]{1,0:T(8,128)(2,1)S(1)}, bf16[176,896]{1,0:T(8,128)(2,1)S(1)}, u32[]{:S(2)}, u32[]{:S(2)}) collective-permute-start(bf16[176,896]{1,0:T(8,128)(2,1)S(1)} %slice.29), channel_id=1, source_target_pairs={{0,2},{4,0},{8,4},{12,8},{14,12},{10,14},{6,10},{2,6},{1,3},{5,1},... | collective-permute-start | bytes 946184 | tf_op jit(solution)/shard_map/ppermute | solution.py:186
  87.7 30.1 %collective-permute-start.28 = (bf16[176,1792]{1,0:T(8,128)(2,1)S(1)}, bf16[176,1792]{1,0:T(8,128)(2,1)S(1)}, u32[]{:S(2)}, u32[]{:S(2)}) collective-permute-start(bf16[176,1792]{1,0:T(8,128)(2,1)S(1)} %shard_map.51.refs_10_.refs_8_), channel_id=1, source_target_pairs={{0,1},{1,0},{2,3},{3,2},{4,5},{5,4},{6,7},{7,6},{8,9},{9,8},{10,11... | collective-permute-start | bytes 1892360 | tf_op jit(solution)/shard_map/ppermute | solution.py:192
  97.6 6.1 %collective-permute-start.14 = (bf16[176,512]{1,0:T(8,128)(2,1)S(1)}, bf16[176,512]{1,0:T(8,128)(2,1)S(1)}, u32[]{:S(2)}, u32[]{:S(2)}) collective-permute-start(bf16[176,512]{1,0:T(8,128)(2,1)S(1)} %collective-permute-done.10.refs_2_), channel_id=1, source_target_pairs={{0,4},{4,8},{8,12},{12,14},{14,10},{10,6},{6,2},{2,0},{1,5},{5,9},... | collective-permute-start | bytes 540680 | tf_op jit(solution)/shard_map/ppermute | solution.py:186
  99.2 5.8 %collective-permute-start.15 = (bf16[176,512]{1,0:T(8,128)(2,1)S(1)}, bf16[176,512]{1,0:T(8,128)(2,1)S(1)}, u32[]{:S(2)}, u32[]{:S(2)}) collective-permute-start(bf16[176,512]{1,0:T(8,128)(2,1)S(1)} %collective-permute-done.11.refs_4_), channel_id=1, source_target_pairs={{0,2},{4,0},{8,4},{12,8},{14,12},{10,14},{6,10},{2,6},{1,3},{5,1},... | collective-permute-start | bytes 540680 | tf_op jit(solution)/shard_map/ppermute | solution.py:186
  99.2 9.0 %collective-permute-start.29 = (bf16[176,512]{1,0:T(8,128)(2,1)S(1)}, bf16[176,512]{1,0:T(8,128)(2,1)S(1)}, u32[]{:S(2)}, u32[]{:S(2)}) collective-permute-start(bf16[176,512]{1,0:T(8,128)(2,1)S(1)} %shard_map.48.refs_0_), channel_id=1, source_target_pairs={{0,1},{1,0},{2,3},{3,2},{4,5},{5,4},{6,7},{7,6},{8,9},{9,8},{10,11... | collective-permute-start | bytes 540680 | tf_op jit(solution)/shard_map/ppermute | solution.py:192
  105.0 4.9 %collective-permute-start.18 = (bf16[176,512]{1,0:T(8,128)(2,1)S(1)}, bf16[176,512]{1,0:T(8,128)(2,1)S(1)}, u32[]{:S(2)}, u32[]{:S(2)}) collective-permute-start(bf16[176,512]{1,0:T(8,128)(2,1)S(1)} %collective-permute-done.14.refs_6_), channel_id=1, source_target_pairs={{0,4},{4,8},{8,12},{12,14},{14,10},{10,6},{6,2},{2,0},{1,5},{5,9},... | collective-permute-start | bytes 540680 | tf_op jit(solution)/shard_map/ppermute | solution.py:186
  105.3 6.6 %collective-permute-start.20 = (bf16[176,512]{1,0:T(8,128)(2,1)S(1)}, bf16[176,512]{1,0:T(8,128)(2,1)S(1)}, u32[]{:S(2)}, u32[]{:S(2)}) collective-permute-start(bf16[176,512]{1,0:T(8,128)(2,1)S(1)} %collective-permute-done.15.refs_8_), channel_id=1, source_target_pairs={{0,2},{4,0},{8,4},{12,8},{14,12},{10,14},{6,10},{2,6},{1,3},{5,1},... | collective-permute-start | bytes 540680 | tf_op jit(solution)/shard_map/ppermute | solution.py:186
  106.5 5.9 %collective-permute-start.31 = (bf16[176,512]{1,0:T(8,128)(2,1)S(1)}, bf16[176,512]{1,0:T(8,128)(2,1)S(1)}, u32[]{:S(2)}, u32[]{:S(2)}) collective-permute-start(bf16[176,512]{1,0:T(8,128)(2,1)S(1)} %collective-permute-done.11.refs_4_), channel_id=1, source_target_pairs={{0,1},{1,0},{2,3},{3,2},{4,5},{5,4},{6,7},{7,6},{8,9},{9,8},{10,11... | collective-permute-start | bytes 540680 | tf_op jit(solution)/shard_map/ppermute | solution.py:192
  112.7 4.7 %collective-permute-start.26 = (bf16[176,256]{1,0:T(8,128)(2,1)S(1)}, bf16[176,256]{1,0:T(8,128)(2,1)S(1)}, u32[]{:S(2)}, u32[]{:S(2)}) collective-permute-start(bf16[176,256]{1,0:T(8,128)(2,1)S(1)} %slice.27), channel_id=1, source_target_pairs={{0,2},{4,0},{8,4},{12,8},{14,12},{10,14},{6,10},{2,6},{1,3},{5,1},... | collective-permute-start | bytes 270344 | tf_op jit(solution)/shard_map/ppermute | solution.py:186
  113.9 6.4 %collective-permute-start.19 = (bf16[176,512]{1,0:T(8,128)(2,1)S(1)}, bf16[176,512]{1,0:T(8,128)(2,1)S(1)}, u32[]{:S(2)}, u32[]{:S(2)}) collective-permute-start(bf16[176,512]{1,0:T(8,128)(2,1)S(1)} %collective-permute-done.18.refs_0_), channel_id=1, source_target_pairs={{0,1},{1,0},{2,3},{3,2},{4,5},{5,4},{6,7},{7,6},{8,9},{9,8},{10,11... | collective-permute-start | bytes 540680 | tf_op jit(solution)/shard_map/ppermute | solution.py:192
  114.6 5.6 %collective-permute-start.21 = (bf16[176,512]{1,0:T(8,128)(2,1)S(1)}, bf16[176,512]{1,0:T(8,128)(2,1)S(1)}, u32[]{:S(2)}, u32[]{:S(2)}) collective-permute-start(bf16[176,512]{1,0:T(8,128)(2,1)S(1)} %collective-permute-done.20.refs_2_), channel_id=1, source_target_pairs={{0,1},{1,0},{2,3},{3,2},{4,5},{5,4},{6,7},{7,6},{8,9},{9,8},{10,11... | collective-permute-start | bytes 540680 | tf_op jit(solution)/shard_map/ppermute | solution.py:192
  (13 other events, 63.4 us)

commit v2 on v1

--- a/solution.py
+++ b/solution.py
@@ -9,6 +9,8 @@
 
 SWAP = ((0, 1), (1, 0))
 SLAB = 448
+WEIGHT = 2
+LATE = 2
 
 
 def chunk_at(n, q):
@@ -20,7 +22,7 @@
     return jnp.where(lax.rem(me, 2) == 0, me // 2, n - 1 - me // 2)
 
 
-def rotate(pieces, distances, offsets, basis, running, last):
+def rotate(pieces, distances, offsets, basis, running, last, weight=WEIGHT):
     count = len(pieces)
     tokens = pieces[0].shape[0]
     columns = basis.shape[1]
@@ -78,7 +80,7 @@
     return pl.pallas_call(
         kernel,
         out_shape=jax.ShapeDtypeStruct((tokens, columns), jnp.bfloat16 if last else jnp.float32),
-        in_specs=[anywhere] * (count + 1 + has_running),
+        in_specs=[pl.BlockSpec(memory_space=pltpu.HBM)] * count + [anywhere] * (1 + has_running),
         out_specs=whole,
         scratch_shapes=[pltpu.VMEM(p.shape, p.dtype) for p in pieces]
         + [
@@ -88,7 +90,9 @@
         ],
         compiler_params=pltpu.CompilerParams(vmem_limit_bytes=planned + 8 * 1024 * 1024),
         cost_estimate=pl.CostEstimate(
-            flops=2 * tokens * total * columns, bytes_accessed=2 * total * columns + 8 * tokens * columns, transcendentals=0
+            flops=2 * weight * tokens * total * columns,
+            bytes_accessed=weight * (2 * total * columns + 8 * tokens * columns),
+            transcendentals=0,
         ),
     )(*pieces, basis, *([running] if has_running else []))
 
@@ -180,46 +184,61 @@
     ahead = [(path[i], path[(i + 1) % n]) for i in range(n)]
     back = [(path[i], path[(i - 1) % n]) for i in range(n)]
 
-    def hop(forward, backward, *after):
-        if after:
-            forward, backward, _ = lax.optimization_barrier((forward, backward, after))
+    def after(values, *gates):
+        return lax.optimization_barrier((tuple(values), gates))[0]
+
+    def hop(values, *gates):
+        forward, backward = after(values, *gates)
         return lax.ppermute(forward, "blk", ahead), lax.ppermute(backward, "blk", back)
 
-    def add(total, got, distance):
-        return rotate(list(got), (-distance, distance), (0, 0), input_basis, total, False)
+    def add(total, pieces, distances, offsets, *gates, last=False, weight=WEIGHT):
+        if gates:
+            pieces = after(pieces, *gates)
+        return rotate(list(pieces), distances, offsets, input_basis, total, last, weight)
 
     def swap(x):
         return lax.ppermute(x, "dp", SWAP)
 
-    g1 = hop(grads, grads)
-    a1 = hop(acts, acts)
-    total = rotate([acts], (0,), (0,), input_basis, None, False)
-    g2 = hop(*g1, total)
-    g3 = hop(*g2)
-    a2 = hop(*a1, g2)
-    total = add(total, a1, 1)
-    g4 = hop(g3[0][:, :half_out], g3[1][:, half_out:], total)
+    low, high = acts[:, :half_in], acts[:, half_in:]
+    first, second = (0, half_in), (half_in, 0)
+    g1 = hop((grads, grads))
+    a1 = hop((low, high))
+    total = add(None, (low, high), (0, 0), first, g1)
+    g2 = hop(g1)
+    b1 = hop((high, low), a1, total)
+    total = add(total, a1, (-1, 1), first, g2)
+    g3 = hop(g2)
+    a2 = hop(a1, b1, total)
+    total = add(total, b1, (-1, 1), second, g3)
+    g4 = hop((g3[0][:, :half_out], g3[1][:, half_out:]))
+    b2 = hop(b1, a2, total)
     rotated_out = rotate(
-        [grads, *g1, *g2, *g3, *g4], (0, -1, 1, -2, 2, -3, 3, -4, 4), (0,) * 8 + (half_out,), output_basis, None, True
-    )
-    r1 = hop(rotated_out, rotated_out)
-    a3 = hop(*a2, g4)
-    total = add(total, a2, 2)
-    r2 = hop(*r1, total)
-    a4 = hop(a3[0][:, :half_in], a3[1][:, half_in:], r1)
-    total = add(total, a3, 3)
-    r3 = hop(*r2, total)
-    rotated_in = rotate(list(a4), (-4, 4), (0, half_in), input_basis, total, True)
-    r4 = hop(r3[0][:, :half_out], r3[1][:, half_out:], rotated_in)
-    other_in = swap(rotated_in)
+        (grads, *g1, *g2, *g3, *g4), (0, -1, 1, -2, 2, -3, 3, -4, 4), (0,) * 8 + (half_out,), output_basis, None, True, 4
+    )
+    r1 = hop((rotated_out, rotated_out))
+    a3 = hop(a2, b2, rotated_out)
+    total = add(total, (*a2, *b2), (-2, 2, -2, 2), (*first, *second), r1, weight=1)
+    r2 = hop(r1)
+    b3 = hop(b2, a3, total)
+    r3 = hop(r2)
+    a4 = hop(a3, b3)
+    total = add(total, (*a3, *b3), (-3, 3, -3, 3), (*first, *second), r3, weight=LATE)
+    r4 = hop((r3[0][:, :half_out], r3[1][:, half_out:]))
+    mine = (rotated_out, *r1, *r2, *r3, *r4)
+    other = [swap(x) for x in (rotated_out, *r1, *r2)]
+    other += [swap(x) for x in after((*r3, *r4), total)]
+    rotated_in = add(total, a4, (-4, 4), first, other[:5], r4, last=True)
     scale = 1.0 / (length * 2)
-
-    def tiles(pieces, distances, offsets, before):
-        pairs = [(p, swap(p)) for p in pieces]
-        return square_tiles(pairs, distances, offsets, rotated_in, other_in, (rows_local, in_width), scale, before)
-
-    out = tiles([rotated_out, *r1, *r2], (0, -1, 1, -2, 2), (0,) * 5, None)
-    return tiles([*r3, *r4], (-3, 3, -4, 4), (0, 0, 0, half_out), out)
+    return square_tiles(
+        list(zip(mine, other)),
+        (0, -1, 1, -2, 2, -3, 3, -4, 4),
+        (0,) * 8 + (half_out,),
+        rotated_in,
+        swap(rotated_in),
+        (rows_local, in_width),
+        scale,
+        None,
+    )
 
 
 def gather_body(activations, out_grads, input_basis, output_basis):

time: 125 us -> 99.5 us (0.80)
  waiting for transfers between devices: 52.1 us -> 21.2 us
  starting transfers between devices: 35.2 us -> 39.8 us
    ppermute x12 -> x15, waiting for transfers between devices: 31.1 us -> 9.13 us  [hop(): lax.ppermute(forward, 'blk', ahead)]
    ppermute x12 -> x15, starting transfers between devices: 10.2 us -> 22.4 us  [hop(): lax.ppermute(forward, 'blk', ahead)]
    ppermute x12 -> x15, waiting for transfers between devices: 20.9 us -> 10.6 us  [hop(): lax.ppermute(backward, 'blk', back)]
    ppermute x12 -> x15, starting transfers between devices: 8.38 us -> 1.7 us  [hop(): lax.ppermute(backward, 'blk', back)]
    ppermute x10, waiting for transfers between devices: 0.03 us -> 1.46 us  [swap(): return lax.ppermute(x, 'dp', SWAP)]
    pallas_call x6 -> x7, Pallas kernels: 29.2 us -> 30.4 us  [rotate(): pl.pallas_call(kernel, out_shape=jax.ShapeDtypeStruct((tokens, columns),...]
    pallas_call x2 -> x1, Pallas kernels: 7.25 us -> 6.42 us  [square_tiles(): pl.pallas_call(kernel, out_shape=jax.ShapeDtypeStruct(shape, jnp.float32)...]
  transfers between devices with their start and end apart: 34 -> 40, of which waited for: 15 -> 20; matrix products, arithmetic and copies ran while one was open for 0% -> 1% of each run, Pallas kernels for 22% -> 27%
where the time goes in v2:
time: 99.5 us; the launch traced here: 99.3 us
  starting transfers between devices  39.8 us (40%)
  Pallas kernels  36.8 us (37%)
  waiting for transfers between devices  21.2 us (21%)
  local copies, waits for them, and re-layouts  1.15 us (1%)
    pallas_call x7, Pallas kernels, rotate(): pl.pallas_call(kernel, out_shape=jax.ShapeDtypeStruct((tokens, columns),...  30.4 us
    ppermute x15, starting transfers between devices, hop(): lax.ppermute(forward, 'blk', ahead)  22.4 us
    ppermute x10, starting transfers between devices, swap(): return lax.ppermute(x, 'dp', SWAP)  15.7 us
    ppermute x15, waiting for transfers between devices, hop(): lax.ppermute(backward, 'blk', back)  10.6 us
    ppermute x15, waiting for transfers between devices, hop(): lax.ppermute(forward, 'blk', ahead)  9.13 us
    pallas_call x1, Pallas kernels, square_tiles(): pl.pallas_call(kernel, out_shape=jax.ShapeDtypeStruct(shape, jnp.float32)...  6.42 us
  transfers between devices with their start and end apart: 40, of which 20 were waited for; matrix products, arithmetic and copies ran while one was open for 1% of the time, Pallas kernels for 27%

profile of v2, /device:TPU:1, one launch (start us, length us, event | category | flops | bytes accessed | tf_op | source)
XLA Modules:
  0.0 99.3 jit_solution(16631302998044026335)
XLA Ops:
  0.0 2.1 %collective-permute-start = (bf16[176,512]{1,0:T(8,128)(2,1)}, bf16[176,512]{1,0:T(8,128)(2,1)S(1)}, u32[]{:S(2)}, u32[]{:S(2)}) collective-permute-start(bf16[176,512]{1,0:T(8,128)(2,1)} %bitcast.2), channel_id=1, source_target_pairs={{0,4},{4,8},{8,12},{12,14},{14,10},{10,6},{6,2},{2,0},{1,5},{5,9},... | collective-permute-start | bytes 540680 | tf_op jit(solution)/shard_map/ppermute | solution.py:192
  3.2 1.5 %collective-permute-start.21 = (bf16[176,896]{1,0:T(8,128)(2,1)S(1)}, bf16[176,896]{1,0:T(8,128)(2,1)S(1)}, u32[]{:S(2)}, u32[]{:S(2)}) collective-permute-start(bf16[176,896]{1,0:T(8,128)(2,1)S(1)} %get-tuple-element.76.refs_0_), channel_id=1, source_target_pairs={{0,4},{4,8},{8,12},{12,14},{14,10},{10,6},{6,2},{2,0},{1,5},{5,9},... | collective-permute-start | bytes 946184 | tf_op jit(solution)/shard_map/ppermute | solution.py:192
  4.8 1.8 %collective-permute-done.refs_1_ = bf16[176,512]{1,0:T(8,128)(2,1)S(1)} collective-permute-done((bf16[176,512]{1,0:T(8,128)(2,1)}, bf16[176,512]{1,0:T(8,128)(2,1)S(1)}, u32[]{:S(2)}, u32[]{:S(2)}) %collective-permute-start) | collective-permute-done | bytes 180256 | tf_op jit(solution)/shard_map/ppermute | solution.py:192
  8.9 3.6 %shard_map.47.refs_3_ = f32[176,1792]{1,0:T(8,128)S(1)} custom-call(bf16[176,896]{1,0:T(8,128)(2,1)S(1)} %get-tuple-element.76.refs_0_, bf16[176,896]{1,0:T(8,128)(2,1)S(1)} %get-tuple-element.75.refs_1_, bf16[14336,1792]{1,0:T(8,128)(2,1)} %refs_2_.7), custom_call_target="tpu_custom_call" | custom-call | flops 2260729856 | bytes 17891328 | tf_op jit(solution)/shard_map/pallas_call | solution.py:80
  19.6 3.8 %shard_map.48.refs_3_ = f32[176,1792]{1,0:T(8,128)S(1)} custom-call(bf16[176,896]{1,0:T(8,128)(2,1)S(1)} %collective-permute-done.21.refs_0_, bf16[176,896]{1,0:T(8,128)(2,1)S(1)} %collective-permute-done.22.refs_1_, bf16[14336,1792]{1,0:T(8,128)(2,1)} %refs_2_.7, f32[176,1792]{1,0:T(8,128)S(1)} %shard_map.47.refs_3_), custom_call_target="tpu_custom_call" | custom-call | flops 2260729856 | bytes 17891328 | tf_op jit(solution)/shard_map/pallas_call | solution.py:80
  25.9 1.5 %collective-permute-done.5.refs_6_ = bf16[176,512]{1,0:T(8,128)(2,1)S(1)} collective-permute-done((bf16[176,512]{1,0:T(8,128)(2,1)S(1)}, bf16[176,512]{1,0:T(8,128)(2,1)S(1)}, u32[]{:S(2)}, u32[]{:S(2)}) %collective-permute-start.5) | collective-permute-done | bytes 180256 | tf_op jit(solution)/shard_map/ppermute | solution.py:192
  29.1 3.8 %shard_map.49.refs_5_ = f32[176,1792]{1,0:T(8,128)S(1)} custom-call(bf16[176,896]{1,0:T(8,128)(2,1)S(1)} %collective-permute-done.23.refs_0_, bf16[176,896]{1,0:T(8,128)(2,1)S(1)} %collective-permute-done.24.refs_1_, bf16[14336,1792]{1,0:T(8,128)(2,1)} %refs_2_.7, f32[176,1792]{1,0:T(8,128)S(1)} %shard_map.48.refs_3_), custom_call_target="tpu_custom_call" | custom-call | flops 2260729856 | bytes 17891328 | tf_op jit(solution)/shard_map/pallas_call | solution.py:80
  35.6 3.7 %shard_map.46.refs_0_ = bf16[176,512]{1,0:T(8,128)(2,1)S(1)} custom-call(bf16[176,512]{1,0:T(8,128)(2,1)S(1)} %bitcast.4, bf16[176,512]{1,0:T(8,128)(2,1)S(1)} %collective-permute-done.refs_1_, bf16[176,512]{1,0:T(8,128)(2,1)S(1)} %collective-permute-done.1.refs_2_, bf16[176,512]{1,0:T(8,128)(2,1)S(1)} %collective-permute-done.2.refs_3_, ...), custom_call_target="tpu_custom_call" | custom-call | flops 2952790016 | bytes 19660800 | tf_op jit(solution)/shard_map/pallas_call | solution.py:80
  41.9 1.6 %collective-permute-start.29 = (bf16[176,896]{1,0:T(8,128)(2,1)S(1)}, bf16[176,896]{1,0:T(8,128)(2,1)S(1)}, u32[]{:S(2)}, u32[]{:S(2)}) collective-permute-start(bf16[176,896]{1,0:T(8,128)(2,1)S(1)} %collective-permute-done.25.refs_0_), channel_id=1, source_target_pairs={{0,4},{4,8},{8,12},{12,14},{14,10},{10,6},{6,2},{2,0},{1,5},{5,9},... | collective-permute-start | bytes 946184 | tf_op jit(solution)/shard_map/ppermute | solution.py:192
  43.5 2.1 %collective-permute-done.9.refs_2_ = bf16[176,512]{1,0:T(8,128)(2,1)S(1)} collective-permute-done((bf16[176,512]{1,0:T(8,128)(2,1)S(1)}, bf16[176,512]{1,0:T(8,128)(2,1)S(1)}, u32[]{:S(2)}, u32[]{:S(2)}) %collective-permute-start.9) | collective-permute-done | bytes 180256 | tf_op jit(solution)/shard_map/ppermute | solution.py:192
  45.6 2.1 %collective-permute-done.11.refs_4_ = bf16[176,512]{1,0:T(8,128)(2,1)S(1)} collective-permute-done((bf16[176,512]{1,0:T(8,128)(2,1)S(1)}, bf16[176,512]{1,0:T(8,128)(2,1)S(1)}, u32[]{:S(2)}, u32[]{:S(2)}) %collective-permute-start.11) | collective-permute-done | bytes 180256 | tf_op jit(solution)/shard_map/ppermute | solution.py:192
  47.7 1.9 %collective-permute-start.13 = (bf16[176,512]{1,0:T(8,128)(2,1)S(1)}, bf16[176,512]{1,0:T(8,128)(2,1)S(1)}, u32[]{:S(2)}, u32[]{:S(2)}) collective-permute-start(bf16[176,512]{1,0:T(8,128)(2,1)S(1)} %collective-permute-done.9.refs_2_), channel_id=1, source_target_pairs={{0,4},{4,8},{8,12},{12,14},{14,10},{10,6},{6,2},{2,0},{1,5},{5,9},... | collective-permute-start | bytes 540680 | tf_op jit(solution)/shard_map/ppermute | solution.py:192
  49.6 5.9 %shard_map.50.refs_5_ = f32[176,1792]{1,0:T(8,128)S(1)} custom-call(bf16[176,896]{1,0:T(8,128)(2,1)S(1)} %collective-permute-done.25.refs_0_, bf16[176,896]{1,0:T(8,128)(2,1)S(1)} %collective-permute-done.26.refs_1_, bf16[176,896]{1,0:T(8,128)(2,1)S(1)} %collective-permute-done.27.refs_2_, bf16[176,896]{1,0:T(8,128)(2,1)S(1)} %collective-permute-done.28.refs_3_, ...), custom_call_target="tpu_custom_call" | custom-call | flops 2260729856 | bytes 15368192 | tf_op jit(solution)/shard_map/pallas_call | solution.py:80
  55.6 1.5 %collective-permute-start.31 = (bf16[176,896]{1,0:T(8,128)(2,1)S(1)}, bf16[176,896]{1,0:T(8,128)(2,1)S(1)}, u32[]{:S(2)}, u32[]{:S(2)}) collective-permute-start(bf16[176,896]{1,0:T(8,128)(2,1)S(1)} %collective-permute-done.27.refs_2_), channel_id=1, source_target_pairs={{0,4},{4,8},{8,12},{12,14},{14,10},{10,6},{6,2},{2,0},{1,5},{5,9},... | collective-permute-start | bytes 946184 | tf_op jit(solution)/shard_map/ppermute | solution.py:192
  57.7 1.6 %collective-permute-start.17 = (bf16[176,512]{1,0:T(8,128)(2,1)S(1)}, bf16[176,512]{1,0:T(8,128)(2,1)S(1)}, u32[]{:S(2)}, u32[]{:S(2)}) collective-permute-start(bf16[176,512]{1,0:T(8,128)(2,1)S(1)} %collective-permute-done.13.refs_6_), channel_id=1, source_target_pairs={{0,4},{4,8},{8,12},{12,14},{14,10},{10,6},{6,2},{2,0},{1,5},{5,9},... | collective-permute-start | bytes 540680 | tf_op jit(solution)/shard_map/ppermute | solution.py:192
  59.3 6.0 %collective-permute-start.8 = (bf16[176,512]{1,0:T(8,128)(2,1)S(1)}, bf16[176,512]{1,0:T(8,128)(2,1)S(1)}, u32[]{:S(2)}, u32[]{:S(2)}) collective-permute-start(bf16[176,512]{1,0:T(8,128)(2,1)S(1)} %shard_map.46.refs_0_), channel_id=1, source_target_pairs={{0,1},{1,0},{2,3},{3,2},{4,5},{5,4},{6,7},{7,6},{8,9},{9,8},{10,11... | collective-permute-start | bytes 540680 | tf_op jit(solution)/shard_map/ppermute | solution.py:200
  65.8 5.0 %collective-permute-start.10 = (bf16[176,512]{1,0:T(8,128)(2,1)S(1)}, bf16[176,512]{1,0:T(8,128)(2,1)S(1)}, u32[]{:S(2)}, u32[]{:S(2)}) collective-permute-start(bf16[176,512]{1,0:T(8,128)(2,1)S(1)} %collective-permute-done.9.refs_2_), channel_id=1, source_target_pairs={{0,1},{1,0},{2,3},{3,2},{4,5},{5,4},{6,7},{7,6},{8,9},{9,8},{10,11... | collective-permute-start | bytes 540680 | tf_op jit(solution)/shard_map/ppermute | solution.py:200
  71.4 1.7 %collective-permute-start.16 = (bf16[176,512]{1,0:T(8,128)(2,1)S(1)}, bf16[176,512]{1,0:T(8,128)(2,1)S(1)}, u32[]{:S(2)}, u32[]{:S(2)}) collective-permute-start(bf16[176,512]{1,0:T(8,128)(2,1)S(1)} %collective-permute-done.15.refs_8_), channel_id=1, source_target_pairs={{0,1},{1,0},{2,3},{3,2},{4,5},{5,4},{6,7},{7,6},{8,9},{9,8},{10,11... | collective-permute-start | bytes 540680 | tf_op jit(solution)/shard_map/ppermute | solution.py:200
  73.1 1.5 %collective-permute-start.19 = (bf16[176,256]{1,0:T(8,128)(2,1)S(1)}, bf16[176,256]{1,0:T(8,128)(2,1)S(1)}, u32[]{:S(2)}, u32[]{:S(2)}) collective-permute-start(bf16[176,256]{1,0:T(8,128)(2,1)S(1)} %slice.26), channel_id=1, source_target_pairs={{0,4},{4,8},{8,12},{12,14},{14,10},{10,6},{6,2},{2,0},{1,5},{5,9},... | collective-permute-start | bytes 270344 | tf_op jit(solution)/shard_map/ppermute | solution.py:192
  74.6 1.5 %collective-permute-start.37 = (bf16[176,896]{1,0:T(8,128)(2,1)S(1)}, bf16[176,896]{1,0:T(8,128)(2,1)S(1)}, u32[]{:S(2)}, u32[]{:S(2)}) collective-permute-start(bf16[176,896]{1,0:T(8,128)(2,1)S(1)} %collective-permute-done.29.refs_0_), channel_id=1, source_target_pairs={{0,4},{4,8},{8,12},{12,14},{14,10},{10,6},{6,2},{2,0},{1,5},{5,9},... | collective-permute-start | bytes 946184 | tf_op jit(solution)/shard_map/ppermute | solution.py:192
  76.3 5.9 %shard_map.51.refs_3_ = f32[176,1792]{1,0:T(8,128)S(1)} custom-call(bf16[176,896]{1,0:T(8,128)(2,1)S(1)} %collective-permute-done.29.refs_0_, bf16[176,896]{1,0:T(8,128)(2,1)S(1)} %collective-permute-done.30.refs_1_, bf16[176,896]{1,0:T(8,128)(2,1)S(1)} %collective-permute-done.31.refs_2_, bf16[176,896]{1,0:T(8,128)(2,1)S(1)} %collective-permute-done.32.refs_3_, ...), custom_call_target="tpu_custom_call" | custom-call | flops 4521459712 | bytes 30736384 | tf_op jit(solution)/shard_map/pallas_call | solution.py:80
  82.3 1.7 %collective-permute-done.37.refs_0_ = bf16[176,896]{1,0:T(8,128)(2,1)S(1)} collective-permute-done((bf16[176,896]{1,0:T(8,128)(2,1)S(1)}, bf16[176,896]{1,0:T(8,128)(2,1)S(1)}, u32[]{:S(2)}, u32[]{:S(2)}) %collective-permute-start.37) | collective-permute-done | bytes 315424 | tf_op jit(solution)/shard_map/ppermute | solution.py:192
  85.1 3.8 %shard_map.52.refs_18_ = bf16[176,1792]{1,0:T(8,128)(2,1)S(1)} custom-call(bf16[176,896]{1,0:T(8,128)(2,1)S(1)} %collective-permute-done.37.refs_0_, bf16[176,896]{1,0:T(8,128)(2,1)S(1)} %collective-permute-done.38.refs_1_, bf16[14336,1792]{1,0:T(8,128)(2,1)} %refs_2_.7, f32[176,1792]{1,0:T(8,128)S(1)} %shard_map.51.refs_3_), custom_call_target="tpu_custom_call" | custom-call | flops 2260729856 | bytes 17891328 | tf_op jit(solution)/shard_map/pallas_call | solution.py:80
  92.7 6.4 %shard_map.53 = f32[2048,1792]{1,0:T(8,128)} custom-call(bf16[176,512]{1,0:T(8,128)(2,1)S(1)} %shard_map.46.refs_0_, bf16[176,512]{1,0:T(8,128)(2,1)S(1)} %collective-permute-done.8.refs_1_, bf16[176,512]{1,0:T(8,128)(2,1)S(1)} %collective-permute-done.9.refs_2_, bf16[176,512]{1,0:T(8,128)(2,1)S(1)} %collective-permute-done.10.refs_3_, ...), custom_call_target="tpu_custom_call" | custom-call | flops 2583691264 | bytes 14680064 | tf_op jit(solution)/shard_map/pallas_call | solution.py:157
  (73 shorter events, 26.9 us)
Async XLA Ops:
  3.2 10.0 %collective-permute-start.21 = (bf16[176,896]{1,0:T(8,128)(2,1)S(1)}, bf16[176,896]{1,0:T(8,128)(2,1)S(1)}, u32[]{:S(2)}, u32[]{:S(2)}) collective-permute-start(bf16[176,896]{1,0:T(8,128)(2,1)S(1)} %get-tuple-element.76.refs_0_), channel_id=1, source_target_pairs={{0,4},{4,8},{8,12},{12,14},{14,10},{10,6},{6,2},{2,0},{1,5},{5,9},... | collective-permute-start | bytes 946184 | tf_op jit(solution)/shard_map/ppermute | solution.py:192
  4.8 9.5 %collective-permute-start.22 = (bf16[176,896]{1,0:T(8,128)(2,1)S(1)}, bf16[176,896]{1,0:T(8,128)(2,1)S(1)}, u32[]{:S(2)}, u32[]{:S(2)}) collective-permute-start(bf16[176,896]{1,0:T(8,128)(2,1)S(1)} %get-tuple-element.75.refs_1_), channel_id=1, source_target_pairs={{0,2},{4,0},{8,4},{12,8},{14,12},{10,14},{6,10},{2,6},{1,3},{5,1},... | collective-permute-start | bytes 946184 | tf_op jit(solution)/shard_map/ppermute | solution.py:192
  7.4 9.7 %collective-permute-start.2 = (bf16[176,512]{1,0:T(8,128)(2,1)S(1)}, bf16[176,512]{1,0:T(8,128)(2,1)S(1)}, u32[]{:S(2)}, u32[]{:S(2)}) collective-permute-start(bf16[176,512]{1,0:T(8,128)(2,1)S(1)} %collective-permute-done.refs_1_), channel_id=1, source_target_pairs={{0,4},{4,8},{8,12},{12,14},{14,10},{10,6},{6,2},{2,0},{1,5},{5,9},... | collective-permute-start | bytes 540680 | tf_op jit(solution)/shard_map/ppermute | solution.py:192
  8.7 9.4 %collective-permute-start.3 = (bf16[176,512]{1,0:T(8,128)(2,1)S(1)}, bf16[176,512]{1,0:T(8,128)(2,1)S(1)}, u32[]{:S(2)}, u32[]{:S(2)}) collective-permute-start(bf16[176,512]{1,0:T(8,128)(2,1)S(1)} %collective-permute-done.1.refs_2_), channel_id=1, source_target_pairs={{0,2},{4,0},{8,4},{12,8},{14,12},{10,14},{6,10},{2,6},{1,3},{5,1},... | collective-permute-start | bytes 540680 | tf_op jit(solution)/shard_map/ppermute | solution.py:192
  14.2 9.1 %collective-permute-start.23 = (bf16[176,896]{1,0:T(8,128)(2,1)S(1)}, bf16[176,896]{1,0:T(8,128)(2,1)S(1)}, u32[]{:S(2)}, u32[]{:S(2)}) collective-permute-start(bf16[176,896]{1,0:T(8,128)(2,1)S(1)} %get-tuple-element.75.refs_1_), channel_id=1, source_target_pairs={{0,4},{4,8},{8,12},{12,14},{14,10},{10,6},{6,2},{2,0},{1,5},{5,9},... | collective-permute-start | bytes 946184 | tf_op jit(solution)/shard_map/ppermute | solution.py:192
  15.5 8.0 %collective-permute-start.24 = (bf16[176,896]{1,0:T(8,128)(2,1)S(1)}, bf16[176,896]{1,0:T(8,128)(2,1)S(1)}, u32[]{:S(2)}, u32[]{:S(2)}) collective-permute-start(bf16[176,896]{1,0:T(8,128)(2,1)S(1)} %get-tuple-element.76.refs_0_), channel_id=1, source_target_pairs={{0,2},{4,0},{8,4},{12,8},{14,12},{10,14},{6,10},{2,6},{1,3},{5,1},... | collective-permute-start | bytes 946184 | tf_op jit(solution)/shard_map/ppermute | solution.py:192
  18.1 7.8 %collective-permute-start.4 = (bf16[176,512]{1,0:T(8,128)(2,1)S(1)}, bf16[176,512]{1,0:T(8,128)(2,1)S(1)}, u32[]{:S(2)}, u32[]{:S(2)}) collective-permute-start(bf16[176,512]{1,0:T(8,128)(2,1)S(1)} %collective-permute-done.2.refs_3_), channel_id=1, source_target_pairs={{0,4},{4,8},{8,12},{12,14},{14,10},{10,6},{6,2},{2,0},{1,5},{5,9},... | collective-permute-start | bytes 540680 | tf_op jit(solution)/shard_map/ppermute | solution.py:192
  19.4 8.0 %collective-permute-start.5 = (bf16[176,512]{1,0:T(8,128)(2,1)S(1)}, bf16[176,512]{1,0:T(8,128)(2,1)S(1)}, u32[]{:S(2)}, u32[]{:S(2)}) collective-permute-start(bf16[176,512]{1,0:T(8,128)(2,1)S(1)} %collective-permute-done.3.refs_4_), channel_id=1, source_target_pairs={{0,2},{4,0},{8,4},{12,8},{14,12},{10,14},{6,10},{2,6},{1,3},{5,1},... | collective-permute-start | bytes 540680 | tf_op jit(solution)/shard_map/ppermute | solution.py:192
  23.5 9.4 %collective-permute-start.25 = (bf16[176,896]{1,0:T(8,128)(2,1)S(1)}, bf16[176,896]{1,0:T(8,128)(2,1)S(1)}, u32[]{:S(2)}, u32[]{:S(2)}) collective-permute-start(bf16[176,896]{1,0:T(8,128)(2,1)S(1)} %collective-permute-done.21.refs_0_), channel_id=1, source_target_pairs={{0,4},{4,8},{8,12},{12,14},{14,10},{10,6},{6,2},{2,0},{1,5},{5,9},... | collective-permute-start | bytes 946184 | tf_op jit(solution)/shard_map/ppermute | solution.py:192
  24.8 8.8 %collective-permute-start.26 = (bf16[176,896]{1,0:T(8,128)(2,1)S(1)}, bf16[176,896]{1,0:T(8,128)(2,1)S(1)}, u32[]{:S(2)}, u32[]{:S(2)}) collective-permute-start(bf16[176,896]{1,0:T(8,128)(2,1)S(1)} %collective-permute-done.22.refs_1_), channel_id=1, source_target_pairs={{0,2},{4,0},{8,4},{12,8},{14,12},{10,14},{6,10},{2,6},{1,3},{5,1},... | collective-permute-start | bytes 946184 | tf_op jit(solution)/shard_map/ppermute | solution.py:192
  41.9 13.6 %collective-permute-start.29 = (bf16[176,896]{1,0:T(8,128)(2,1)S(1)}, bf16[176,896]{1,0:T(8,128)(2,1)S(1)}, u32[]{:S(2)}, u32[]{:S(2)}) collective-permute-start(bf16[176,896]{1,0:T(8,128)(2,1)S(1)} %collective-permute-done.25.refs_0_), channel_id=1, source_target_pairs={{0,4},{4,8},{8,12},{12,14},{14,10},{10,6},{6,2},{2,0},{1,5},{5,9},... | collective-permute-start | bytes 946184 | tf_op jit(solution)/shard_map/ppermute | solution.py:192
  43.5 12.0 %collective-permute-start.30 = (bf16[176,896]{1,0:T(8,128)(2,1)S(1)}, bf16[176,896]{1,0:T(8,128)(2,1)S(1)}, u32[]{:S(2)}, u32[]{:S(2)}) collective-permute-start(bf16[176,896]{1,0:T(8,128)(2,1)S(1)} %collective-permute-done.26.refs_1_), channel_id=1, source_target_pairs={{0,2},{4,0},{8,4},{12,8},{14,12},{10,14},{6,10},{2,6},{1,3},{5,1},... | collective-permute-start | bytes 946184 | tf_op jit(solution)/shard_map/ppermute | solution.py:192
  47.7 9.3 %collective-permute-start.13 = (bf16[176,512]{1,0:T(8,128)(2,1)S(1)}, bf16[176,512]{1,0:T(8,128)(2,1)S(1)}, u32[]{:S(2)}, u32[]{:S(2)}) collective-permute-start(bf16[176,512]{1,0:T(8,128)(2,1)S(1)} %collective-permute-done.9.refs_2_), channel_id=1, source_target_pairs={{0,4},{4,8},{8,12},{12,14},{14,10},{10,6},{6,2},{2,0},{1,5},{5,9},... | collective-permute-start | bytes 540680 | tf_op jit(solution)/shard_map/ppermute | solution.py:192
  49.6 8.0 %collective-permute-start.15 = (bf16[176,512]{1,0:T(8,128)(2,1)S(1)}, bf16[176,512]{1,0:T(8,128)(2,1)S(1)}, u32[]{:S(2)}, u32[]{:S(2)}) collective-permute-start(bf16[176,512]{1,0:T(8,128)(2,1)S(1)} %collective-permute-done.11.refs_4_), channel_id=1, source_target_pairs={{0,2},{4,0},{8,4},{12,8},{14,12},{10,14},{6,10},{2,6},{1,3},{5,1},... | collective-permute-start | bytes 540680 | tf_op jit(solution)/shard_map/ppermute | solution.py:192
  55.6 15.3 %collective-permute-start.31 = (bf16[176,896]{1,0:T(8,128)(2,1)S(1)}, bf16[176,896]{1,0:T(8,128)(2,1)S(1)}, u32[]{:S(2)}, u32[]{:S(2)}) collective-permute-start(bf16[176,896]{1,0:T(8,128)(2,1)S(1)} %collective-permute-done.27.refs_2_), channel_id=1, source_target_pairs={{0,4},{4,8},{8,12},{12,14},{14,10},{10,6},{6,2},{2,0},{1,5},{5,9},... | collective-permute-start | bytes 946184 | tf_op jit(solution)/shard_map/ppermute | solution.py:192
  57.7 8.2 %collective-permute-start.17 = (bf16[176,512]{1,0:T(8,128)(2,1)S(1)}, bf16[176,512]{1,0:T(8,128)(2,1)S(1)}, u32[]{:S(2)}, u32[]{:S(2)}) collective-permute-start(bf16[176,512]{1,0:T(8,128)(2,1)S(1)} %collective-permute-done.13.refs_6_), channel_id=1, source_target_pairs={{0,4},{4,8},{8,12},{12,14},{14,10},{10,6},{6,2},{2,0},{1,5},{5,9},... | collective-permute-start | bytes 540680 | tf_op jit(solution)/shard_map/ppermute | solution.py:192
  59.3 11.6 %collective-permute-start.18 = (bf16[176,512]{1,0:T(8,128)(2,1)S(1)}, bf16[176,512]{1,0:T(8,128)(2,1)S(1)}, u32[]{:S(2)}, u32[]{:S(2)}) collective-permute-start(bf16[176,512]{1,0:T(8,128)(2,1)S(1)} %collective-permute-done.15.refs_8_), channel_id=1, source_target_pairs={{0,2},{4,0},{8,4},{12,8},{14,12},{10,14},{6,10},{2,6},{1,3},{5,1},... | collective-permute-start | bytes 540680 | tf_op jit(solution)/shard_map/ppermute | solution.py:192
  59.3 12.1 %collective-permute-start.32 = (bf16[176,896]{1,0:T(8,128)(2,1)S(1)}, bf16[176,896]{1,0:T(8,128)(2,1)S(1)}, u32[]{:S(2)}, u32[]{:S(2)}) collective-permute-start(bf16[176,896]{1,0:T(8,128)(2,1)S(1)} %collective-permute-done.28.refs_3_), channel_id=1, source_target_pairs={{0,2},{4,0},{8,4},{12,8},{14,12},{10,14},{6,10},{2,6},{1,3},{5,1},... | collective-permute-start | bytes 946184 | tf_op jit(solution)/shard_map/ppermute | solution.py:192
  59.3 13.8 %collective-permute-start.8 = (bf16[176,512]{1,0:T(8,128)(2,1)S(1)}, bf16[176,512]{1,0:T(8,128)(2,1)S(1)}, u32[]{:S(2)}, u32[]{:S(2)}) collective-permute-start(bf16[176,512]{1,0:T(8,128)(2,1)S(1)} %shard_map.46.refs_0_), channel_id=1, source_target_pairs={{0,1},{1,0},{2,3},{3,2},{4,5},{5,4},{6,7},{7,6},{8,9},{9,8},{10,11... | collective-permute-start | bytes 540680 | tf_op jit(solution)/shard_map/ppermute | solution.py:200
  65.8 8.8 %collective-permute-start.10 = (bf16[176,512]{1,0:T(8,128)(2,1)S(1)}, bf16[176,512]{1,0:T(8,128)(2,1)S(1)}, u32[]{:S(2)}, u32[]{:S(2)}) collective-permute-start(bf16[176,512]{1,0:T(8,128)(2,1)S(1)} %collective-permute-done.9.refs_2_), channel_id=1, source_target_pairs={{0,1},{1,0},{2,3},{3,2},{4,5},{5,4},{6,7},{7,6},{8,9},{9,8},{10,11... | collective-permute-start | bytes 540680 | tf_op jit(solution)/shard_map/ppermute | solution.py:200
  71.4 10.8 %collective-permute-start.16 = (bf16[176,512]{1,0:T(8,128)(2,1)S(1)}, bf16[176,512]{1,0:T(8,128)(2,1)S(1)}, u32[]{:S(2)}, u32[]{:S(2)}) collective-permute-start(bf16[176,512]{1,0:T(8,128)(2,1)S(1)} %collective-permute-done.15.refs_8_), channel_id=1, source_target_pairs={{0,1},{1,0},{2,3},{3,2},{4,5},{5,4},{6,7},{7,6},{8,9},{9,8},{10,11... | collective-permute-start | bytes 540680 | tf_op jit(solution)/shard_map/ppermute | solution.py:200
  73.1 9.1 %collective-permute-start.19 = (bf16[176,256]{1,0:T(8,128)(2,1)S(1)}, bf16[176,256]{1,0:T(8,128)(2,1)S(1)}, u32[]{:S(2)}, u32[]{:S(2)}) collective-permute-start(bf16[176,256]{1,0:T(8,128)(2,1)S(1)} %slice.26), channel_id=1, source_target_pairs={{0,4},{4,8},{8,12},{12,14},{14,10},{10,6},{6,2},{2,0},{1,5},{5,9},... | collective-permute-start | bytes 270344 | tf_op jit(solution)/shard_map/ppermute | solution.py:192
  74.6 9.4 %collective-permute-start.37 = (bf16[176,896]{1,0:T(8,128)(2,1)S(1)}, bf16[176,896]{1,0:T(8,128)(2,1)S(1)}, u32[]{:S(2)}, u32[]{:S(2)}) collective-permute-start(bf16[176,896]{1,0:T(8,128)(2,1)S(1)} %collective-permute-done.29.refs_0_), channel_id=1, source_target_pairs={{0,4},{4,8},{8,12},{12,14},{14,10},{10,6},{6,2},{2,0},{1,5},{5,9},... | collective-permute-start | bytes 946184 | tf_op jit(solution)/shard_map/ppermute | solution.py:192
  76.1 9.0 %collective-permute-start.38 = (bf16[176,896]{1,0:T(8,128)(2,1)S(1)}, bf16[176,896]{1,0:T(8,128)(2,1)S(1)}, u32[]{:S(2)}, u32[]{:S(2)}) collective-permute-start(bf16[176,896]{1,0:T(8,128)(2,1)S(1)} %collective-permute-done.30.refs_1_), channel_id=1, source_target_pairs={{0,2},{4,0},{8,4},{12,8},{14,12},{10,14},{6,10},{2,6},{1,3},{5,1},... | collective-permute-start | bytes 946184 | tf_op jit(solution)/shard_map/ppermute | solution.py:192
  (18 other events, 99.3 us)

commit v3 on v2

--- a/solution.py
+++ b/solution.py
@@ -10,7 +10,7 @@
 SWAP = ((0, 1), (1, 0))
 SLAB = 448
 WEIGHT = 2
-LATE = 2
+LATE = 1
 
 
 def chunk_at(n, q):
@@ -220,14 +220,14 @@
     total = add(total, (*a2, *b2), (-2, 2, -2, 2), (*first, *second), r1, weight=1)
     r2 = hop(r1)
     b3 = hop(b2, a3, total)
-    r3 = hop(r2)
+    r3 = hop(r2, total)
     a4 = hop(a3, b3)
-    total = add(total, (*a3, *b3), (-3, 3, -3, 3), (*first, *second), r3, weight=LATE)
+    total = add(total, a3, (-3, 3), first, r2, weight=2)
+    total = add(total, b3, (-3, 3), second, r3, weight=2)
     r4 = hop((r3[0][:, :half_out], r3[1][:, half_out:]))
     mine = (rotated_out, *r1, *r2, *r3, *r4)
-    other = [swap(x) for x in (rotated_out, *r1, *r2)]
-    other += [swap(x) for x in after((*r3, *r4), total)]
-    rotated_in = add(total, a4, (-4, 4), first, other[:5], r4, last=True)
+    other = [swap(x) for x in mine]
+    rotated_in = add(total, a4, (-4, 4), first, other, last=True)
     scale = 1.0 / (length * 2)
     return square_tiles(
         list(zip(mine, other)),

time: 99.5 us -> 98 us (0.985)
  waiting for transfers between devices: 21.2 us -> 18.6 us
  Pallas kernels: 36.8 us -> 38.5 us
    ppermute x15, waiting for transfers between devices: 9.13 us -> 7.41 us  [hop(): lax.ppermute(forward, 'blk', ahead)]
    pallas_call x7 -> x8, Pallas kernels: 30.4 us -> 32.1 us  [rotate(): pl.pallas_call(kernel, out_shape=jax.ShapeDtypeStruct((tokens, columns),...]
    ppermute x15, waiting for transfers between devices: 10.6 us -> 9.53 us  [hop(): lax.ppermute(backward, 'blk', back)]
  transfers between devices with their start and end apart: 40 -> 40, of which waited for: 20 -> 17; matrix products, arithmetic and copies ran while one was open for 1% -> 1% of each run, Pallas kernels for 27% -> 29%
where the time goes in v3:
time: 98 us; the launch traced here: 97.8 us
  starting transfers between devices  39.2 us (40%)
  Pallas kernels  38.5 us (39%)
  waiting for transfers between devices  18.6 us (19%)
  local copies, waits for them, and re-layouts  1.15 us (1%)
    pallas_call x8, Pallas kernels, rotate(): pl.pallas_call(kernel, out_shape=jax.ShapeDtypeStruct((tokens, columns),...  32.1 us
    ppermute x15, starting transfers between devices, hop(): lax.ppermute(forward, 'blk', ahead)  22.1 us
    ppermute x10, starting transfers between devices, swap(): return lax.ppermute(x, 'dp', SWAP)  15.3 us
    ppermute x15, waiting for transfers between devices, hop(): lax.ppermute(backward, 'blk', back)  9.53 us
    ppermute x15, waiting for transfers between devices, hop(): lax.ppermute(forward, 'blk', ahead)  7.41 us
    pallas_call x1, Pallas kernels, square_tiles(): pl.pallas_call(kernel, out_shape=jax.ShapeDtypeStruct(shape, jnp.float32)...  6.34 us
  transfers between devices with their start and end apart: 40, of which 17 were waited for; matrix products, arithmetic and copies ran while one was open for 1% of the time, Pallas kernels for 29%

profile of v3, /device:TPU:1, one launch (start us, length us, event | category | flops | bytes accessed | tf_op | source)
XLA Modules:
  0.0 97.8 jit_solution(4137433898456406797)
XLA Ops:
  0.0 2.1 %collective-permute-start = (bf16[176,512]{1,0:T(8,128)(2,1)}, bf16[176,512]{1,0:T(8,128)(2,1)S(1)}, u32[]{:S(2)}, u32[]{:S(2)}) collective-permute-start(bf16[176,512]{1,0:T(8,128)(2,1)} %bitcast.2), channel_id=1, source_target_pairs={{0,4},{4,8},{8,12},{12,14},{14,10},{10,6},{6,2},{2,0},{1,5},{5,9},... | collective-permute-start | bytes 540680 | tf_op jit(solution)/shard_map/ppermute | solution.py:192
  3.2 1.5 %collective-permute-start.17 = (bf16[176,896]{1,0:T(8,128)(2,1)S(1)}, bf16[176,896]{1,0:T(8,128)(2,1)S(1)}, u32[]{:S(2)}, u32[]{:S(2)}) collective-permute-start(bf16[176,896]{1,0:T(8,128)(2,1)S(1)} %get-tuple-element.68.refs_0_), channel_id=1, source_target_pairs={{0,4},{4,8},{8,12},{12,14},{14,10},{10,6},{6,2},{2,0},{1,5},{5,9},... | collective-permute-start | bytes 946184 | tf_op jit(solution)/shard_map/ppermute | solution.py:192
  4.8 1.8 %collective-permute-done.refs_1_ = bf16[176,512]{1,0:T(8,128)(2,1)S(1)} collective-permute-done((bf16[176,512]{1,0:T(8,128)(2,1)}, bf16[176,512]{1,0:T(8,128)(2,1)S(1)}, u32[]{:S(2)}, u32[]{:S(2)}) %collective-permute-start) | collective-permute-done | bytes 180256 | tf_op jit(solution)/shard_map/ppermute | solution.py:192
  8.9 3.6 %shard_map.47.refs_3_ = f32[176,1792]{1,0:T(8,128)S(1)} custom-call(bf16[176,896]{1,0:T(8,128)(2,1)S(1)} %get-tuple-element.68.refs_0_, bf16[176,896]{1,0:T(8,128)(2,1)S(1)} %get-tuple-element.67.refs_1_, bf16[14336,1792]{1,0:T(8,128)(2,1)} %refs_2_.11), custom_call_target="tpu_custom_call" | custom-call | flops 2260729856 | bytes 17891328 | tf_op jit(solution)/shard_map/pallas_call | solution.py:80
  15.7 1.4 %collective-permute-done.2.refs_3_ = bf16[176,512]{1,0:T(8,128)(2,1)S(1)} collective-permute-done((bf16[176,512]{1,0:T(8,128)(2,1)S(1)}, bf16[176,512]{1,0:T(8,128)(2,1)S(1)}, u32[]{:S(2)}, u32[]{:S(2)}) %collective-permute-start.2) | collective-permute-done | bytes 180256 | tf_op jit(solution)/shard_map/ppermute | solution.py:192
  19.6 3.8 %shard_map.48.refs_3_ = f32[176,1792]{1,0:T(8,128)S(1)} custom-call(bf16[176,896]{1,0:T(8,128)(2,1)S(1)} %collective-permute-done.17.refs_0_, bf16[176,896]{1,0:T(8,128)(2,1)S(1)} %collective-permute-done.18.refs_1_, bf16[14336,1792]{1,0:T(8,128)(2,1)} %refs_2_.11, f32[176,1792]{1,0:T(8,128)S(1)} %shard_map.47.refs_3_), custom_call_target="tpu_custom_call" | custom-call | flops 2260729856 | bytes 17891328 | tf_op jit(solution)/shard_map/pallas_call | solution.py:80
  25.9 1.5 %collective-permute-done.5.refs_6_ = bf16[176,512]{1,0:T(8,128)(2,1)S(1)} collective-permute-done((bf16[176,512]{1,0:T(8,128)(2,1)S(1)}, bf16[176,512]{1,0:T(8,128)(2,1)S(1)}, u32[]{:S(2)}, u32[]{:S(2)}) %collective-permute-start.5) | collective-permute-done | bytes 180256 | tf_op jit(solution)/shard_map/ppermute | solution.py:192
  27.4 1.3 %collective-permute-start.6 = (bf16[176,256]{1,0:T(8,128)(2,1)S(1)}, bf16[176,256]{1,0:T(8,128)(2,1)S(1)}, u32[]{:S(2)}, u32[]{:S(2)}) collective-permute-start(bf16[176,256]{1,0:T(8,128)(2,1)S(1)} %slice.24), channel_id=1, source_target_pairs={{0,4},{4,8},{8,12},{12,14},{14,10},{10,6},{6,2},{2,0},{1,5},{5,9},... | collective-permute-start | bytes 270344 | tf_op jit(solution)/shard_map/ppermute | solution.py:192
  29.1 3.8 %shard_map.49.refs_5_ = f32[176,1792]{1,0:T(8,128)S(1)} custom-call(bf16[176,896]{1,0:T(8,128)(2,1)S(1)} %collective-permute-done.19.refs_0_, bf16[176,896]{1,0:T(8,128)(2,1)S(1)} %collective-permute-done.20.refs_1_, bf16[14336,1792]{1,0:T(8,128)(2,1)} %refs_2_.11, f32[176,1792]{1,0:T(8,128)S(1)} %shard_map.48.refs_3_), custom_call_target="tpu_custom_call" | custom-call | flops 2260729856 | bytes 17891328 | tf_op jit(solution)/shard_map/pallas_call | solution.py:80
  35.6 3.7 %shard_map.46.refs_0_ = bf16[176,512]{1,0:T(8,128)(2,1)S(1)} custom-call(bf16[176,512]{1,0:T(8,128)(2,1)S(1)} %bitcast.4, bf16[176,512]{1,0:T(8,128)(2,1)S(1)} %collective-permute-done.refs_1_, bf16[176,512]{1,0:T(8,128)(2,1)S(1)} %collective-permute-done.1.refs_2_, bf16[176,512]{1,0:T(8,128)(2,1)S(1)} %collective-permute-done.2.refs_3_, ...), custom_call_target="tpu_custom_call" | custom-call | flops 2952790016 | bytes 19660800 | tf_op jit(solution)/shard_map/pallas_call | solution.py:80
  41.9 1.6 %collective-permute-start.33 = (bf16[176,896]{1,0:T(8,128)(2,1)S(1)}, bf16[176,896]{1,0:T(8,128)(2,1)S(1)}, u32[]{:S(2)}, u32[]{:S(2)}) collective-permute-start(bf16[176,896]{1,0:T(8,128)(2,1)S(1)} %collective-permute-done.21.refs_0_), channel_id=1, source_target_pairs={{0,4},{4,8},{8,12},{12,14},{14,10},{10,6},{6,2},{2,0},{1,5},{5,9},... | collective-permute-start | bytes 946184 | tf_op jit(solution)/shard_map/ppermute | solution.py:192
  43.5 2.1 %collective-permute-done.9.refs_2_ = bf16[176,512]{1,0:T(8,128)(2,1)S(1)} collective-permute-done((bf16[176,512]{1,0:T(8,128)(2,1)S(1)}, bf16[176,512]{1,0:T(8,128)(2,1)S(1)}, u32[]{:S(2)}, u32[]{:S(2)}) %collective-permute-start.9) | collective-permute-done | bytes 180256 | tf_op jit(solution)/shard_map/ppermute | solution.py:192
  45.6 2.1 %collective-permute-done.11.refs_4_ = bf16[176,512]{1,0:T(8,128)(2,1)S(1)} collective-permute-done((bf16[176,512]{1,0:T(8,128)(2,1)S(1)}, bf16[176,512]{1,0:T(8,128)(2,1)S(1)}, u32[]{:S(2)}, u32[]{:S(2)}) %collective-permute-start.11) | collective-permute-done | bytes 180256 | tf_op jit(solution)/shard_map/ppermute | solution.py:192
  47.7 1.9 %collective-permute-start.13 = (bf16[176,512]{1,0:T(8,128)(2,1)S(1)}, bf16[176,512]{1,0:T(8,128)(2,1)S(1)}, u32[]{:S(2)}, u32[]{:S(2)}) collective-permute-start(bf16[176,512]{1,0:T(8,128)(2,1)S(1)} %collective-permute-done.9.refs_2_), channel_id=1, source_target_pairs={{0,4},{4,8},{8,12},{12,14},{14,10},{10,6},{6,2},{2,0},{1,5},{5,9},... | collective-permute-start | bytes 540680 | tf_op jit(solution)/shard_map/ppermute | solution.py:192
  49.6 5.9 %shard_map.50.refs_3_ = f32[176,1792]{1,0:T(8,128)S(1)} custom-call(bf16[176,896]{1,0:T(8,128)(2,1)S(1)} %collective-permute-done.21.refs_0_, bf16[176,896]{1,0:T(8,128)(2,1)S(1)} %collective-permute-done.22.refs_1_, bf16[176,896]{1,0:T(8,128)(2,1)S(1)} %collective-permute-done.23.refs_2_, bf16[176,896]{1,0:T(8,128)(2,1)S(1)} %collective-permute-done.24.refs_3_, ...), custom_call_target="tpu_custom_call" | custom-call | flops 2260729856 | bytes 15368192 | tf_op jit(solution)/shard_map/pallas_call | solution.py:80
  55.6 1.5 %collective-permute-start.35 = (bf16[176,896]{1,0:T(8,128)(2,1)S(1)}, bf16[176,896]{1,0:T(8,128)(2,1)S(1)}, u32[]{:S(2)}, u32[]{:S(2)}) collective-permute-start(bf16[176,896]{1,0:T(8,128)(2,1)S(1)} %collective-permute-done.23.refs_2_), channel_id=1, source_target_pairs={{0,4},{4,8},{8,12},{12,14},{14,10},{10,6},{6,2},{2,0},{1,5},{5,9},... | collective-permute-start | bytes 946184 | tf_op jit(solution)/shard_map/ppermute | solution.py:192
  57.7 1.6 %collective-permute-start.25 = (bf16[176,512]{1,0:T(8,128)(2,1)S(1)}, bf16[176,512]{1,0:T(8,128)(2,1)S(1)}, u32[]{:S(2)}, u32[]{:S(2)}) collective-permute-start(bf16[176,512]{1,0:T(8,128)(2,1)S(1)} %collective-permute-done.13.refs_6_), channel_id=1, source_target_pairs={{0,4},{4,8},{8,12},{12,14},{14,10},{10,6},{6,2},{2,0},{1,5},{5,9},... | collective-permute-start | bytes 540680 | tf_op jit(solution)/shard_map/ppermute | solution.py:192
  59.3 6.0 %collective-permute-start.8 = (bf16[176,512]{1,0:T(8,128)(2,1)S(1)}, bf16[176,512]{1,0:T(8,128)(2,1)S(1)}, u32[]{:S(2)}, u32[]{:S(2)}) collective-permute-start(bf16[176,512]{1,0:T(8,128)(2,1)S(1)} %shard_map.46.refs_0_), channel_id=1, source_target_pairs={{0,1},{1,0},{2,3},{3,2},{4,5},{5,4},{6,7},{7,6},{8,9},{9,8},{10,11... | collective-permute-start | bytes 540680 | tf_op jit(solution)/shard_map/ppermute | solution.py:200
  65.8 5.0 %collective-permute-start.10 = (bf16[176,512]{1,0:T(8,128)(2,1)S(1)}, bf16[176,512]{1,0:T(8,128)(2,1)S(1)}, u32[]{:S(2)}, u32[]{:S(2)}) collective-permute-start(bf16[176,512]{1,0:T(8,128)(2,1)S(1)} %collective-permute-done.9.refs_2_), channel_id=1, source_target_pairs={{0,1},{1,0},{2,3},{3,2},{4,5},{5,4},{6,7},{7,6},{8,9},{9,8},{10,11... | collective-permute-start | bytes 540680 | tf_op jit(solution)/shard_map/ppermute | solution.py:200
  76.1 3.8 %shard_map.51.refs_3_ = f32[176,1792]{1,0:T(8,128)S(1)} custom-call(bf16[176,896]{1,0:T(8,128)(2,1)S(1)} %collective-permute-done.33.refs_0_, bf16[176,896]{1,0:T(8,128)(2,1)S(1)} %collective-permute-done.34.refs_1_, bf16[14336,1792]{1,0:T(8,128)(2,1)} %refs_2_.11, f32[176,1792]{1,0:T(8,128)S(1)} %shard_map.50.refs_3_), custom_call_target="tpu_custom_call" | custom-call | flops 2260729856 | bytes 17891328 | tf_op jit(solution)/shard_map/pallas_call | solution.py:80
  81.1 3.8 %shard_map.52.refs_3_ = f32[176,1792]{1,0:T(8,128)S(1)} custom-call(bf16[176,896]{1,0:T(8,128)(2,1)S(1)} %collective-permute-done.35.refs_0_, bf16[176,896]{1,0:T(8,128)(2,1)S(1)} %collective-permute-done.36.refs_1_, bf16[14336,1792]{1,0:T(8,128)(2,1)} %refs_2_.11, f32[176,1792]{1,0:T(8,128)S(1)} %shard_map.51.refs_3_), custom_call_target="tpu_custom_call" | custom-call | flops 2260729856 | bytes 17891328 | tf_op jit(solution)/shard_map/pallas_call | solution.py:80
  84.9 3.8 %shard_map.53.refs_18_ = bf16[176,1792]{1,0:T(8,128)(2,1)S(1)} custom-call(bf16[176,896]{1,0:T(8,128)(2,1)S(1)} %collective-permute-done.37.refs_0_, bf16[176,896]{1,0:T(8,128)(2,1)S(1)} %collective-permute-done.38.refs_1_, bf16[14336,1792]{1,0:T(8,128)(2,1)} %refs_2_.11, f32[176,1792]{1,0:T(8,128)S(1)} %shard_map.52.refs_3_), custom_call_target="tpu_custom_call" | custom-call | flops 2260729856 | bytes 17891328 | tf_op jit(solution)/shard_map/pallas_call | solution.py:80
  89.6 1.7 %collective-permute-done.39.refs_19_ = bf16[176,1792]{1,0:T(8,128)(2,1)S(1)} collective-permute-done((bf16[176,1792]{1,0:T(8,128)(2,1)S(1)}, bf16[176,1792]{1,0:T(8,128)(2,1)S(1)}, u32[]{:S(2)}, u32[]{:S(2)}) %collective-permute-start.39) | collective-permute-done | bytes 630816 | tf_op jit(solution)/shard_map/ppermute | solution.py:200
  91.3 6.3 %shard_map.54 = f32[2048,1792]{1,0:T(8,128)} custom-call(bf16[176,512]{1,0:T(8,128)(2,1)S(1)} %shard_map.46.refs_0_, bf16[176,512]{1,0:T(8,128)(2,1)S(1)} %collective-permute-done.8.refs_1_, bf16[176,512]{1,0:T(8,128)(2,1)S(1)} %collective-permute-done.9.refs_2_, bf16[176,512]{1,0:T(8,128)(2,1)S(1)} %collective-permute-done.10.refs_3_, ...), custom_call_target="tpu_custom_call" | custom-call | flops 2583691264 | bytes 14680064 | tf_op jit(solution)/shard_map/pallas_call | solution.py:157
  (74 shorter events, 25.7 us)
Async XLA Ops:
  3.2 10.0 %collective-permute-start.17 = (bf16[176,896]{1,0:T(8,128)(2,1)S(1)}, bf16[176,896]{1,0:T(8,128)(2,1)S(1)}, u32[]{:S(2)}, u32[]{:S(2)}) collective-permute-start(bf16[176,896]{1,0:T(8,128)(2,1)S(1)} %get-tuple-element.68.refs_0_), channel_id=1, source_target_pairs={{0,4},{4,8},{8,12},{12,14},{14,10},{10,6},{6,2},{2,0},{1,5},{5,9},... | collective-permute-start | bytes 946184 | tf_op jit(solution)/shard_map/ppermute | solution.py:192
  4.8 9.5 %collective-permute-start.18 = (bf16[176,896]{1,0:T(8,128)(2,1)S(1)}, bf16[176,896]{1,0:T(8,128)(2,1)S(1)}, u32[]{:S(2)}, u32[]{:S(2)}) collective-permute-start(bf16[176,896]{1,0:T(8,128)(2,1)S(1)} %get-tuple-element.67.refs_1_), channel_id=1, source_target_pairs={{0,2},{4,0},{8,4},{12,8},{14,12},{10,14},{6,10},{2,6},{1,3},{5,1},... | collective-permute-start | bytes 946184 | tf_op jit(solution)/shard_map/ppermute | solution.py:192
  7.4 9.7 %collective-permute-start.2 = (bf16[176,512]{1,0:T(8,128)(2,1)S(1)}, bf16[176,512]{1,0:T(8,128)(2,1)S(1)}, u32[]{:S(2)}, u32[]{:S(2)}) collective-permute-start(bf16[176,512]{1,0:T(8,128)(2,1)S(1)} %collective-permute-done.refs_1_), channel_id=1, source_target_pairs={{0,4},{4,8},{8,12},{12,14},{14,10},{10,6},{6,2},{2,0},{1,5},{5,9},... | collective-permute-start | bytes 540680 | tf_op jit(solution)/shard_map/ppermute | solution.py:192
  8.7 9.4 %collective-permute-start.3 = (bf16[176,512]{1,0:T(8,128)(2,1)S(1)}, bf16[176,512]{1,0:T(8,128)(2,1)S(1)}, u32[]{:S(2)}, u32[]{:S(2)}) collective-permute-start(bf16[176,512]{1,0:T(8,128)(2,1)S(1)} %collective-permute-done.1.refs_2_), channel_id=1, source_target_pairs={{0,2},{4,0},{8,4},{12,8},{14,12},{10,14},{6,10},{2,6},{1,3},{5,1},... | collective-permute-start | bytes 540680 | tf_op jit(solution)/shard_map/ppermute | solution.py:192
  14.2 9.1 %collective-permute-start.19 = (bf16[176,896]{1,0:T(8,128)(2,1)S(1)}, bf16[176,896]{1,0:T(8,128)(2,1)S(1)}, u32[]{:S(2)}, u32[]{:S(2)}) collective-permute-start(bf16[176,896]{1,0:T(8,128)(2,1)S(1)} %get-tuple-element.67.refs_1_), channel_id=1, source_target_pairs={{0,4},{4,8},{8,12},{12,14},{14,10},{10,6},{6,2},{2,0},{1,5},{5,9},... | collective-permute-start | bytes 946184 | tf_op jit(solution)/shard_map/ppermute | solution.py:192
  15.5 8.0 %collective-permute-start.20 = (bf16[176,896]{1,0:T(8,128)(2,1)S(1)}, bf16[176,896]{1,0:T(8,128)(2,1)S(1)}, u32[]{:S(2)}, u32[]{:S(2)}) collective-permute-start(bf16[176,896]{1,0:T(8,128)(2,1)S(1)} %get-tuple-element.68.refs_0_), channel_id=1, source_target_pairs={{0,2},{4,0},{8,4},{12,8},{14,12},{10,14},{6,10},{2,6},{1,3},{5,1},... | collective-permute-start | bytes 946184 | tf_op jit(solution)/shard_map/ppermute | solution.py:192
  18.1 7.8 %collective-permute-start.4 = (bf16[176,512]{1,0:T(8,128)(2,1)S(1)}, bf16[176,512]{1,0:T(8,128)(2,1)S(1)}, u32[]{:S(2)}, u32[]{:S(2)}) collective-permute-start(bf16[176,512]{1,0:T(8,128)(2,1)S(1)} %collective-permute-done.2.refs_3_), channel_id=1, source_target_pairs={{0,4},{4,8},{8,12},{12,14},{14,10},{10,6},{6,2},{2,0},{1,5},{5,9},... | collective-permute-start | bytes 540680 | tf_op jit(solution)/shard_map/ppermute | solution.py:192
  19.4 8.0 %collective-permute-start.5 = (bf16[176,512]{1,0:T(8,128)(2,1)S(1)}, bf16[176,512]{1,0:T(8,128)(2,1)S(1)}, u32[]{:S(2)}, u32[]{:S(2)}) collective-permute-start(bf16[176,512]{1,0:T(8,128)(2,1)S(1)} %collective-permute-done.3.refs_4_), channel_id=1, source_target_pairs={{0,2},{4,0},{8,4},{12,8},{14,12},{10,14},{6,10},{2,6},{1,3},{5,1},... | collective-permute-start | bytes 540680 | tf_op jit(solution)/shard_map/ppermute | solution.py:192
  23.5 9.4 %collective-permute-start.21 = (bf16[176,896]{1,0:T(8,128)(2,1)S(1)}, bf16[176,896]{1,0:T(8,128)(2,1)S(1)}, u32[]{:S(2)}, u32[]{:S(2)}) collective-permute-start(bf16[176,896]{1,0:T(8,128)(2,1)S(1)} %collective-permute-done.17.refs_0_), channel_id=1, source_target_pairs={{0,4},{4,8},{8,12},{12,14},{14,10},{10,6},{6,2},{2,0},{1,5},{5,9},... | collective-permute-start | bytes 946184 | tf_op jit(solution)/shard_map/ppermute | solution.py:192
  24.8 8.8 %collective-permute-start.22 = (bf16[176,896]{1,0:T(8,128)(2,1)S(1)}, bf16[176,896]{1,0:T(8,128)(2,1)S(1)}, u32[]{:S(2)}, u32[]{:S(2)}) collective-permute-start(bf16[176,896]{1,0:T(8,128)(2,1)S(1)} %collective-permute-done.18.refs_1_), channel_id=1, source_target_pairs={{0,2},{4,0},{8,4},{12,8},{14,12},{10,14},{6,10},{2,6},{1,3},{5,1},... | collective-permute-start | bytes 946184 | tf_op jit(solution)/shard_map/ppermute | solution.py:192
  27.4 7.7 %collective-permute-start.6 = (bf16[176,256]{1,0:T(8,128)(2,1)S(1)}, bf16[176,256]{1,0:T(8,128)(2,1)S(1)}, u32[]{:S(2)}, u32[]{:S(2)}) collective-permute-start(bf16[176,256]{1,0:T(8,128)(2,1)S(1)} %slice.24), channel_id=1, source_target_pairs={{0,4},{4,8},{8,12},{12,14},{14,10},{10,6},{6,2},{2,0},{1,5},{5,9},... | collective-permute-start | bytes 270344 | tf_op jit(solution)/shard_map/ppermute | solution.py:192
  41.9 13.6 %collective-permute-start.33 = (bf16[176,896]{1,0:T(8,128)(2,1)S(1)}, bf16[176,896]{1,0:T(8,128)(2,1)S(1)}, u32[]{:S(2)}, u32[]{:S(2)}) collective-permute-start(bf16[176,896]{1,0:T(8,128)(2,1)S(1)} %collective-permute-done.21.refs_0_), channel_id=1, source_target_pairs={{0,4},{4,8},{8,12},{12,14},{14,10},{10,6},{6,2},{2,0},{1,5},{5,9},... | collective-permute-start | bytes 946184 | tf_op jit(solution)/shard_map/ppermute | solution.py:192
  43.5 12.0 %collective-permute-start.34 = (bf16[176,896]{1,0:T(8,128)(2,1)S(1)}, bf16[176,896]{1,0:T(8,128)(2,1)S(1)}, u32[]{:S(2)}, u32[]{:S(2)}) collective-permute-start(bf16[176,896]{1,0:T(8,128)(2,1)S(1)} %collective-permute-done.22.refs_1_), channel_id=1, source_target_pairs={{0,2},{4,0},{8,4},{12,8},{14,12},{10,14},{6,10},{2,6},{1,3},{5,1},... | collective-permute-start | bytes 946184 | tf_op jit(solution)/shard_map/ppermute | solution.py:192
  47.7 9.3 %collective-permute-start.13 = (bf16[176,512]{1,0:T(8,128)(2,1)S(1)}, bf16[176,512]{1,0:T(8,128)(2,1)S(1)}, u32[]{:S(2)}, u32[]{:S(2)}) collective-permute-start(bf16[176,512]{1,0:T(8,128)(2,1)S(1)} %collective-permute-done.9.refs_2_), channel_id=1, source_target_pairs={{0,4},{4,8},{8,12},{12,14},{14,10},{10,6},{6,2},{2,0},{1,5},{5,9},... | collective-permute-start | bytes 540680 | tf_op jit(solution)/shard_map/ppermute | solution.py:192
  49.6 8.0 %collective-permute-start.15 = (bf16[176,512]{1,0:T(8,128)(2,1)S(1)}, bf16[176,512]{1,0:T(8,128)(2,1)S(1)}, u32[]{:S(2)}, u32[]{:S(2)}) collective-permute-start(bf16[176,512]{1,0:T(8,128)(2,1)S(1)} %collective-permute-done.11.refs_4_), channel_id=1, source_target_pairs={{0,2},{4,0},{8,4},{12,8},{14,12},{10,14},{6,10},{2,6},{1,3},{5,1},... | collective-permute-start | bytes 540680 | tf_op jit(solution)/shard_map/ppermute | solution.py:192
  55.6 16.3 %collective-permute-start.35 = (bf16[176,896]{1,0:T(8,128)(2,1)S(1)}, bf16[176,896]{1,0:T(8,128)(2,1)S(1)}, u32[]{:S(2)}, u32[]{:S(2)}) collective-permute-start(bf16[176,896]{1,0:T(8,128)(2,1)S(1)} %collective-permute-done.23.refs_2_), channel_id=1, source_target_pairs={{0,4},{4,8},{8,12},{12,14},{14,10},{10,6},{6,2},{2,0},{1,5},{5,9},... | collective-permute-start | bytes 946184 | tf_op jit(solution)/shard_map/ppermute | solution.py:192
  57.1 14.8 %collective-permute-start.36 = (bf16[176,896]{1,0:T(8,128)(2,1)S(1)}, bf16[176,896]{1,0:T(8,128)(2,1)S(1)}, u32[]{:S(2)}, u32[]{:S(2)}) collective-permute-start(bf16[176,896]{1,0:T(8,128)(2,1)S(1)} %collective-permute-done.24.refs_3_), channel_id=1, source_target_pairs={{0,2},{4,0},{8,4},{12,8},{14,12},{10,14},{6,10},{2,6},{1,3},{5,1},... | collective-permute-start | bytes 946184 | tf_op jit(solution)/shard_map/ppermute | solution.py:192
  57.7 8.2 %collective-permute-start.25 = (bf16[176,512]{1,0:T(8,128)(2,1)S(1)}, bf16[176,512]{1,0:T(8,128)(2,1)S(1)}, u32[]{:S(2)}, u32[]{:S(2)}) collective-permute-start(bf16[176,512]{1,0:T(8,128)(2,1)S(1)} %collective-permute-done.13.refs_6_), channel_id=1, source_target_pairs={{0,4},{4,8},{8,12},{12,14},{14,10},{10,6},{6,2},{2,0},{1,5},{5,9},... | collective-permute-start | bytes 540680 | tf_op jit(solution)/shard_map/ppermute | solution.py:192
  59.3 11.6 %collective-permute-start.27 = (bf16[176,512]{1,0:T(8,128)(2,1)S(1)}, bf16[176,512]{1,0:T(8,128)(2,1)S(1)}, u32[]{:S(2)}, u32[]{:S(2)}) collective-permute-start(bf16[176,512]{1,0:T(8,128)(2,1)S(1)} %collective-permute-done.15.refs_8_), channel_id=1, source_target_pairs={{0,2},{4,0},{8,4},{12,8},{14,12},{10,14},{6,10},{2,6},{1,3},{5,1},... | collective-permute-start | bytes 540680 | tf_op jit(solution)/shard_map/ppermute | solution.py:192
  59.3 13.1 %collective-permute-start.8 = (bf16[176,512]{1,0:T(8,128)(2,1)S(1)}, bf16[176,512]{1,0:T(8,128)(2,1)S(1)}, u32[]{:S(2)}, u32[]{:S(2)}) collective-permute-start(bf16[176,512]{1,0:T(8,128)(2,1)S(1)} %shard_map.46.refs_0_), channel_id=1, source_target_pairs={{0,1},{1,0},{2,3},{3,2},{4,5},{5,4},{6,7},{7,6},{8,9},{9,8},{10,11... | collective-permute-start | bytes 540680 | tf_op jit(solution)/shard_map/ppermute | solution.py:200
  65.8 7.9 %collective-permute-start.10 = (bf16[176,512]{1,0:T(8,128)(2,1)S(1)}, bf16[176,512]{1,0:T(8,128)(2,1)S(1)}, u32[]{:S(2)}, u32[]{:S(2)}) collective-permute-start(bf16[176,512]{1,0:T(8,128)(2,1)S(1)} %collective-permute-done.9.refs_2_), channel_id=1, source_target_pairs={{0,1},{1,0},{2,3},{3,2},{4,5},{5,4},{6,7},{7,6},{8,9},{9,8},{10,11... | collective-permute-start | bytes 540680 | tf_op jit(solution)/shard_map/ppermute | solution.py:200
  72.4 7.4 %collective-permute-start.29 = (bf16[176,256]{1,0:T(8,128)(2,1)S(1)}, bf16[176,256]{1,0:T(8,128)(2,1)S(1)}, u32[]{:S(2)}, u32[]{:S(2)}) collective-permute-start(bf16[176,256]{1,0:T(8,128)(2,1)S(1)} %slice.28), channel_id=1, source_target_pairs={{0,4},{4,8},{8,12},{12,14},{14,10},{10,6},{6,2},{2,0},{1,5},{5,9},... | collective-permute-start | bytes 270344 | tf_op jit(solution)/shard_map/ppermute | solution.py:192
  74.6 10.3 %collective-permute-start.37 = (bf16[176,896]{1,0:T(8,128)(2,1)S(1)}, bf16[176,896]{1,0:T(8,128)(2,1)S(1)}, u32[]{:S(2)}, u32[]{:S(2)}) collective-permute-start(bf16[176,896]{1,0:T(8,128)(2,1)S(1)} %collective-permute-done.33.refs_0_), channel_id=1, source_target_pairs={{0,4},{4,8},{8,12},{12,14},{14,10},{10,6},{6,2},{2,0},{1,5},{5,9},... | collective-permute-start | bytes 946184 | tf_op jit(solution)/shard_map/ppermute | solution.py:192
  75.9 9.0 %collective-permute-start.38 = (bf16[176,896]{1,0:T(8,128)(2,1)S(1)}, bf16[176,896]{1,0:T(8,128)(2,1)S(1)}, u32[]{:S(2)}, u32[]{:S(2)}) collective-permute-start(bf16[176,896]{1,0:T(8,128)(2,1)S(1)} %collective-permute-done.34.refs_1_), channel_id=1, source_target_pairs={{0,2},{4,0},{8,4},{12,8},{14,12},{10,14},{6,10},{2,6},{1,3},{5,1},... | collective-permute-start | bytes 946184 | tf_op jit(solution)/shard_map/ppermute | solution.py:192
  (18 other events, 102.0 us)
